TPU v7x, 256 devices: a whole 4x4x8 slice. The times are simulated.
256 devices in a mesh: slab: 8 (over y, core), blk: 32 (over x, z).
Axes of the slice: x: 4, y: 4, z: 8, core: 2. Of those that a mesh axis runs over, the one named last changes fastest.
Arguments:
- fine_in: bfloat16 [3072, 64, 512], P(('slab', 'blk')), may hold values from -6 to 6
- latent: bfloat16 [8, 32, 16, 256], P('slab', 'blk'), may hold values from -6 to 6
- w_fine: bfloat16 [448, 64], replicated, may hold values from -0.25 to 0.25
- w_down: bfloat16 [512, 256], replicated, may hold values from -2 to 2
- w_coarse: bfloat16 [6912, 256], replicated, may hold values from -0.078125 to 0.078125
- w_up: bfloat16 [256, 512], replicated, may hold values from -0.09375 to 0.09375
- neighbors: int32 [3072, 6], P(('slab', 'blk')), may hold values from -1 to 3071, as said below
- pool_owner: int32 [3072, 1], P(('slab', 'blk')), may hold values from 0 to 31; in each aligned block of 12 rows (0 to 11, 12 to 23, ...) at most 2 rows name the same one
- pool_cell: int32 [3072], P(('slab', 'blk')), may hold values from 0 to 15
- cot_fine: bfloat16 [3072, 64, 512], P(('slab', 'blk')), may hold values from -6 to 6
- cot_coarse: bfloat16 [8, 32, 16, 256], P('slab', 'blk'), may hold values from -6 to 6
Outputs:
- fine_out: bfloat16 [3072, 64, 512], P(('slab', 'blk'))
- coarse_out: bfloat16 [8, 32, 16, 256], P('slab', 'blk')
- grad_fine: bfloat16 [3072, 64, 512], P(('slab', 'blk'))
- grad_latent: bfloat16 [8, 32, 16, 256], P('slab', 'blk')
- weight_grads: float32 [2060288], P(('slab', 'blk'))
Inputs may be any that keep to these rules, and one draw needn't show every extreme that they name: Blocks 12 k to 12 k + 11 belong to device k in slab+blk order. neighbors[b, d] = n >= 0 exactly when neighbors[n, d xor 1] = b; n lies on the same device as b or on the previous or next device; from each device to each of its neighbouring devices go at most 6 faces, exactly 6 except from the ends. `pool_owner`: among the 12 blocks of one device at most 2 name one owner, and that bound is reached.
All inputs are finite; a program needn't handle non-finite values.
Results may differ from a plain program's by a relative error of at most 0.013.
Values may be sent and summed in bfloat16 or wider, within the bound.
A program may use at most 128 MiB of HBM per device.

v0:
```python
import math

import jax
import jax.numpy as jnp
import numpy as np
from jax import lax
from jax.sharding import PartitionSpec as P

FB = 6


OPPOSITE = (1, 0, 3, 2, 5, 4)
STRIDES = (64, 8, 1)


def extended_2(cells, sides, width):
    for axis, dim in sides:
        count = lax.axis_size(axis)
        ends = count - 1
        head = lax.slice_in_dim(cells, 0, width, axis=dim)
        tail = lax.slice_in_dim(cells, cells.shape[dim] - width, cells.shape[dim], axis=dim)
        cells = jnp.concatenate(
            [
                lax.ppermute(tail, axis, [(i, (i + 1) % count) for i in range(ends)]),
                cells,
                lax.ppermute(head, axis, [((i + 1) % count, i) for i in range(ends)]),
            ],
            axis=dim,
        )
    return cells


def voxel_tables():
    voxel = np.arange(512)
    coords = (voxel // 64, voxel // 8 % 8, voxel % 8)
    octant = 4 * (coords[0] // 4) + 2 * (coords[1] // 4) + coords[2] // 4
    octant_table = (octant[:, None] == np.arange(8)[None, :]).astype(np.float32)
    placing = np.zeros((6, 64, 512), np.float32)
    edges = np.zeros((6, 512), bool)
    for axis_id in range(3):
        others = [coords[other] for other in range(3) if other != axis_id]
        face_index = others[0] * 8 + others[1]
        for side_id in range(2):
            onface = coords[axis_id] == 7 * side_id
            placing[2 * axis_id + side_id, face_index[onface], voxel[onface]] = 1.0
            edges[2 * axis_id + side_id] = onface
    return (octant_table, placing, edges)


def octant_sum(tensor):
    count_b, channels = (tensor.shape[0], tensor.shape[1])
    octant_table = voxel_tables()[0]
    flat = tensor.reshape(count_b * channels, 512)
    summed = jnp.dot(
        flat, jnp.asarray(octant_table, jnp.bfloat16), preferred_element_type=jnp.float32
    )
    return summed.reshape(count_b, channels * 8)


def octant_expand(values, channels):
    count_b = values.shape[0]
    octant_table = voxel_tables()[0]
    flat = values.reshape(count_b * channels, 8)
    spread = jnp.dot(
        flat,
        jnp.asarray(octant_table.T, jnp.float32),
        precision=lax.Precision.HIGHEST,
        preferred_element_type=jnp.float32,
    )
    return spread.reshape(count_b, channels, 512)


def block_faces(tensor):
    placing = voxel_tables()[1]
    faces = jnp.einsum(
        "bcv,dkv->bdck",
        tensor,
        jnp.asarray(placing, jnp.bfloat16),
        preferred_element_type=jnp.float32,
    )
    return faces.astype(jnp.bfloat16)


def shifted(tensor, nearby_faces):
    count_b, channels = (tensor.shape[0], tensor.shape[1])
    placing, edges = (voxel_tables()[1], voxel_tables()[2])
    moved_list = []
    for axis_id in range(3):
        stride = STRIDES[axis_id]
        filler = jnp.zeros((count_b, channels, stride), tensor.dtype)
        for side_id in range(2):
            direction = 2 * axis_id + side_id
            if side_id == 1:
                moved = jnp.concatenate([tensor[:, :, stride:], filler], axis=2)
            else:
                moved = jnp.concatenate([filler, tensor[:, :, : 512 - stride]], axis=2)
            placed = jnp.einsum(
                "bck,kv->bcv",
                nearby_faces[:, direction],
                jnp.asarray(placing[direction], jnp.bfloat16),
                preferred_element_type=jnp.float32,
            ).astype(jnp.bfloat16)
            onface = jnp.asarray(edges[direction])[None, None, :]
            moved_list.append(jnp.where(onface, placed, moved))
    return moved_list


def silu_slope(values):
    sigmoid = jax.nn.sigmoid(values)
    return sigmoid * (1.0 + values * (1.0 - sigmoid))


def coarse_conv(padded, weight):
    planes, rows_y, columns = (padded.shape[0] - 2, padded.shape[1] - 2, padded.shape[2] - 2)
    width_c = padded.shape[3]
    result = jnp.zeros((planes * rows_y * columns, weight.shape[1]), jnp.float32)
    for step_z in range(3):
        for step_y in range(3):
            joined = jnp.concatenate(
                [
                    padded[
                        step_z : step_z + planes,
                        step_y : step_y + rows_y,
                        step_x : step_x + columns,
                    ]
                    for step_x in range(3)
                ],
                axis=-1,
            ).reshape(-1, 3 * width_c)
            offset = (step_z * 3 + step_y) * 3 * width_c
            result = result + jnp.dot(
                joined, weight[offset : offset + 3 * width_c], preferred_element_type=jnp.float32
            )
    return result.reshape(planes, rows_y, columns, weight.shape[1])


def coarse_transpose(padded_grad, weight):
    planes, rows_y, columns = (
        padded_grad.shape[0] - 2,
        padded_grad.shape[1] - 2,
        padded_grad.shape[2] - 2,
    )
    width_c = padded_grad.shape[3]
    result = jnp.zeros((planes * rows_y * columns, width_c), jnp.float32)
    for step_z in range(3):
        for step_y in range(3):
            joined = jnp.concatenate(
                [
                    padded_grad[
                        2 - step_z : 2 - step_z + planes,
                        2 - step_y : 2 - step_y + rows_y,
                        2 - step_x : 2 - step_x + columns,
                    ]
                    for step_x in range(3)
                ],
                axis=-1,
            ).reshape(-1, 3 * width_c)
            offset = (step_z * 3 + step_y) * 3 * width_c
            block_w = (
                weight[offset : offset + 3 * width_c]
                .reshape(3, width_c, width_c)
                .transpose(0, 2, 1)
                .reshape(3 * width_c, width_c)
            )
            result = result + jnp.dot(joined, block_w, preferred_element_type=jnp.float32)
    return result.reshape(planes, rows_y, columns, width_c)


def coarse_weight_grad(padded, grad_pre):
    planes, rows_y, columns = (padded.shape[0] - 2, padded.shape[1] - 2, padded.shape[2] - 2)
    width_c = padded.shape[3]
    flat_grad = grad_pre.reshape(-1, grad_pre.shape[3])
    pieces = []
    for step_z in range(3):
        for step_y in range(3):
            joined = jnp.concatenate(
                [
                    padded[
                        step_z : step_z + planes,
                        step_y : step_y + rows_y,
                        step_x : step_x + columns,
                    ]
                    for step_x in range(3)
                ],
                axis=-1,
            ).reshape(-1, 3 * width_c)
            pieces.append(
                lax.dot_general(
                    joined, flat_grad, (((0,), (0,)), ((), ())), preferred_element_type=jnp.float32
                )
            )
    return jnp.concatenate(pieces, axis=0)


def fine_conv(tap_list, weight):
    channels = tap_list[0].shape[1]
    result = jnp.zeros(tap_list[0].shape, jnp.float32)
    for tap_id in range(7):
        block_w = weight[tap_id * channels : (tap_id + 1) * channels]
        result = result + jnp.einsum(
            "bkv,ko->bov", tap_list[tap_id], block_w, preferred_element_type=jnp.float32
        )
    return result


def fine_transpose(grad_pre, back_list, weight):
    channels = grad_pre.shape[1]
    result = jnp.einsum(
        "bov,ko->bkv", grad_pre, weight[0:channels], preferred_element_type=jnp.float32
    )
    for direction in range(6):
        block_w = weight[(direction + 1) * channels : (direction + 2) * channels]
        result = result + jnp.einsum(
            "bov,ko->bkv",
            back_list[OPPOSITE[direction]],
            block_w,
            preferred_element_type=jnp.float32,
        )
    return result


def fine_weight_grad(tap_list, grad_pre):
    pieces = []
    for tap_id in range(7):
        pieces.append(
            jnp.einsum(
                "bkv,bov->ko", tap_list[tap_id], grad_pre, preferred_element_type=jnp.float32
            )
        )
    return jnp.concatenate(pieces, axis=0)


def rimmed(tensor):
    extended = extended_2(tensor, (("slab", 0), ("blk", 1)), 1)
    return jnp.pad(extended, ((0, 0), (0, 0), (1, 1), (0, 0)))


def swap_rows(packed):
    returned = lax.all_to_all(packed, "blk", split_axis=0, concat_axis=0, tiled=True)
    return returned.reshape(packed.shape[0] * packed.shape[1], packed.shape[2])


def shards(
    fine_in,
    latent,
    w_fine,
    w_down,
    w_coarse,
    w_up,
    neighbors,
    pool_owner,
    pool_cell,
    cot_fine,
    cot_coarse,
):
    blocks, channels = (fine_in.shape[0], fine_in.shape[1])
    width_c = latent.shape[3]
    owners = lax.axis_size("blk")
    devices = lax.axis_size(("slab", "blk"))
    position = lax.axis_index(("slab", "blk"))
    capacity = max(2, 3 * blocks // owners)
    face_count = blocks * 6
    opposite = jnp.array(OPPOSITE, jnp.int32)
    present = neighbors >= 0
    relation = jnp.where(present, neighbors // blocks - position, 5).reshape(-1)
    lookup = (jnp.where(present, neighbors % blocks, 0) * 6 + opposite[None, :]).reshape(-1)
    slot_ids = jnp.arange(FB, dtype=jnp.int32)
    senders = []
    ranking = []
    for step_dev in (-1, 1):
        chosen = relation == step_dev
        counter = jnp.cumsum(chosen.astype(jnp.int32)) - 1
        senders.append((counter[None, :] == slot_ids[:, None]) & chosen[None, :])
        earlier = (lookup[None, :] < lookup[:, None]) & chosen[None, :]
        ranking.append(jnp.sum(earlier.astype(jnp.int32), axis=1))
    send_pick = jnp.stack(senders).astype(jnp.bfloat16)
    column = jnp.where(
        relation == 0,
        lookup,
        jnp.where(
            relation == -1,
            face_count + ranking[0],
            jnp.where(relation == 1, face_count + FB + ranking[1], -1),
        ),
    )
    near_pick = (
        column[:, None] == jnp.arange(face_count + 2 * FB, dtype=jnp.int32)[None, :]
    ).astype(jnp.bfloat16)

    def nearby(tensor):
        face_rows = block_faces(tensor).reshape(face_count, channels * 64)
        outgoing = jnp.einsum(
            "sqf,fx->sqx", send_pick, face_rows, preferred_element_type=jnp.float32
        ).astype(jnp.bfloat16)
        arrived = extended_2(outgoing, ((("slab", "blk"), 0),), 1)
        face_table = jnp.concatenate([face_rows, arrived[0], arrived[3]], axis=0)
        gathered = jnp.dot(near_pick, face_table, preferred_element_type=jnp.float32).astype(
            jnp.bfloat16
        )
        return gathered.reshape(blocks, 6, channels, 64)

    owner_ids = pool_owner[:, 0]
    member = (owner_ids[:, None] == jnp.arange(owners, dtype=jnp.int32)[None, :]).astype(jnp.int32)
    placed = jnp.sum((jnp.cumsum(member, axis=0) - 1) * member, axis=1)
    slot_of = owner_ids * capacity + placed
    routing = jnp.arange(owners * capacity, dtype=jnp.int32)[:, None] == slot_of[None, :]
    route_pick = routing.astype(jnp.bfloat16)
    sent_cells = jnp.sum(jnp.where(routing, pool_cell[None, :] + 1, 0), axis=1) - 1
    got_cells = lax.all_to_all(
        sent_cells.reshape(owners, capacity), "blk", split_axis=0, concat_axis=0, tiled=True
    ).reshape(-1)
    cell_count = latent.shape[0] * latent.shape[1] * latent.shape[2]
    scatter_pick = (jnp.arange(cell_count, dtype=jnp.int32)[:, None] == got_cells[None, :]).astype(
        jnp.bfloat16
    )

    def to_owners(row_block):
        packed = jnp.dot(route_pick, row_block, preferred_element_type=jnp.float32).astype(
            jnp.bfloat16
        )
        arrived_rows = swap_rows(packed.reshape(owners, capacity, width_c))
        return jnp.dot(scatter_pick, arrived_rows, preferred_element_type=jnp.float32).reshape(
            latent.shape
        )

    def from_cells(grid_flat):
        packed = lax.dot_general(
            scatter_pick, grid_flat, (((0,), (0,)), ((), ())), preferred_element_type=jnp.float32
        ).astype(jnp.bfloat16)
        returned = swap_rows(packed.reshape(owners, capacity, width_c))
        return lax.dot_general(
            route_pick, returned, (((0,), (0,)), ((), ())), preferred_element_type=jnp.float32
        ).astype(jnp.bfloat16)

    tap_list = [fine_in] + shifted(fine_in, nearby(fine_in))
    pre_fine = fine_conv(tap_list, w_fine)
    fine_mid = (fine_in.astype(jnp.float32) + jax.nn.silu(pre_fine)).astype(jnp.bfloat16)
    octant_means = (octant_sum(fine_mid) / 64.0).astype(jnp.bfloat16)
    pooled = jnp.dot(octant_means, w_down, preferred_element_type=jnp.float32).astype(jnp.bfloat16)
    coarse_in = (latent.astype(jnp.float32) + to_owners(pooled)).astype(jnp.bfloat16)
    padded = rimmed(coarse_in)
    pre_coarse = coarse_conv(padded, w_coarse)
    coarse_out = (coarse_in.astype(jnp.float32) + jax.nn.silu(pre_coarse)).astype(jnp.bfloat16)
    lifted = from_cells(coarse_out.reshape(cell_count, width_c))
    raised = jnp.dot(lifted, w_up, preferred_element_type=jnp.float32)
    fine_out = (fine_mid.astype(jnp.float32) + octant_expand(raised, channels)).astype(jnp.bfloat16)
    d_raised = octant_sum(cot_fine).astype(jnp.bfloat16)
    grad_up = lax.dot_general(
        lifted, d_raised, (((0,), (0,)), ((), ())), preferred_element_type=jnp.float32
    )
    d_lifted = lax.dot_general(
        d_raised, w_up, (((1,), (1,)), ((), ())), preferred_element_type=jnp.float32
    ).astype(jnp.bfloat16)
    d_coarse_out = cot_coarse.astype(jnp.float32) + to_owners(d_lifted)
    d_pre_coarse = (d_coarse_out * silu_slope(pre_coarse)).astype(jnp.bfloat16)
    grad_coarse_w = coarse_weight_grad(padded, d_pre_coarse)
    d_coarse_in = d_coarse_out + coarse_transpose(rimmed(d_pre_coarse), w_coarse)
    grad_latent = d_coarse_in.astype(jnp.bfloat16)
    d_pooled = from_cells(grad_latent.reshape(cell_count, width_c))
    grad_down = lax.dot_general(
        octant_means, d_pooled, (((0,), (0,)), ((), ())), preferred_element_type=jnp.float32
    )
    d_means = lax.dot_general(
        d_pooled, w_down, (((1,), (1,)), ((), ())), preferred_element_type=jnp.float32
    )
    d_mid = cot_fine.astype(jnp.float32) + octant_expand(d_means, channels) / 64.0
    d_pre_fine = (d_mid * silu_slope(pre_fine)).astype(jnp.bfloat16)
    back_list = shifted(d_pre_fine, nearby(d_pre_fine))
    grad_fine = (d_mid + fine_transpose(d_pre_fine, back_list, w_fine)).astype(jnp.bfloat16)
    grad_fine_w = fine_weight_grad(tap_list, d_pre_fine)
    total_rows = blocks * devices
    all_cells = cell_count * devices
    flat_grads = jnp.concatenate(
        [
            grad_fine_w.reshape(-1) / math.sqrt(total_rows * 512),
            grad_down.reshape(-1) / math.sqrt(total_rows),
            grad_coarse_w.reshape(-1) / math.sqrt(all_cells),
            grad_up.reshape(-1) / math.sqrt(total_rows),
        ]
    )
    weight_grads = lax.psum_scatter(flat_grads, ("slab", "blk"), scatter_dimension=0, tiled=True)
    return (fine_out, coarse_out, grad_fine, grad_latent, weight_grads)


def solution(mesh):
    return jax.shard_map(
        shards,
        mesh=mesh,
        in_specs=(
            P(("slab", "blk"), None, None),
            P("slab", "blk", None, None),
            P(),
            P(),
            P(),
            P(),
            P(("slab", "blk"), None),
            P(("slab", "blk"), None),
            P(("slab", "blk")),
            P(("slab", "blk"), None, None),
            P("slab", "blk", None, None),
        ),
        out_specs=(
            P(("slab", "blk"), None, None),
            P("slab", "blk", None, None),
            P(("slab", "blk"), None, None),
            P("slab", "blk", None, None),
            P(("slab", "blk")),
        ),
        check_vma=False,
    )
```

profile of v0, /device:TPU:32, one launch (start us, length us, event | category | flops | bytes accessed | tf_op | source)
XLA Modules:
  0.0 541.6 jit_solution(17114302771519924181)
XLA Ops:
  10.3 11.2 %all-to-all-start = ((s32[32,1,2]{2,1,0:T(1,128)}), s32[32,1,2]{2,1,0:T(1,128)}, u32[]{:S(2)}, u32[]{:S(2)}) async-start(s32[32,1,2]{2,1,0:T(1,128)} %bitcast.33), calls=%async_computation | async-start | bytes 32768 | tf_op jit(solution)/shard_map/all_to_all | solution.py:309
  23.5 3.1 fusion.1
  26.6 1.7 copy.186
  30.0 3.4 collective-permute-start
  33.4 2.8 collective-permute-start.1
  36.2 1.5 fusion.220
  37.7 1.5 fusion.219
  41.1 1.5 fusion.120
  42.9 1.7 reshape.497
  46.3 1.6 convolution_convert_fusion.1
  47.9 2.3 reshape.498
  60.6 2.2 add_convert_fusion.1
  63.7 1.5 copy.198
  65.2 1.8 convert_element_type.206
  67.0 1.9 convolution_convert_fusion.21
  70.2 11.0 %all-to-all-start.1 = ((bf16[32,2,256]{2,1,0:T(2,128)(2,1)}), bf16[32,2,256]{2,1,0:T(2,128)(2,1)}, u32[]{:S(2)}, u32[]{:S(2)}) async-start(bf16[32,2,256]{2,1,0:T(2,128)(2,1)} %reshape.500), calls=%async_computation.1 | async-start | bytes 65536 | tf_op jit(solution)/shard_map/all_to_all | solution.py:239
  81.3 1.6 convolution_convert_fusion.19
  84.8 2.0 reduce.7
  87.7 2.5 all-to-all-done.1
  90.1 7.4 %all-to-all-start.3 = ((bf16[32,2,256]{2,1,0:T(2,128)(2,1)}), bf16[32,2,256]{2,1,0:T(2,128)(2,1)}, u32[]{:S(2)}, u32[]{:S(2)}) async-start(bf16[32,2,256]{2,1,0:T(2,128)(2,1)} %reshape.516), calls=%async_computation.3 | async-start | bytes 65536 | tf_op jit(solution)/shard_map/all_to_all | solution.py:239
  97.5 1.4 reshape.501
  101.1 3.6 collective-permute-start.2
  104.7 3.8 fusion.214
  108.5 1.9 copy.209
  110.4 1.9 copy.207
  112.3 1.9 copy.206
  114.2 1.9 copy.205
  116.1 1.9 copy.204
  118.1 1.9 copy.203
  120.0 1.9 copy.202
  121.9 1.9 copy.201
  123.8 1.9 copy.208
  125.8 1.4 reshape.517
  127.9 2.2 collective-permute-start.5
  130.1 4.1 collective-permute-start.4
  149.0 3.6 collective-permute-start.6
  156.0 11.3 %all-to-all-start.2 = ((bf16[32,2,256]{2,1,0:T(2,128)(2,1)}), bf16[32,2,256]{2,1,0:T(2,128)(2,1)}, u32[]{:S(2)}, u32[]{:S(2)}) async-start(bf16[32,2,256]{2,1,0:T(2,128)(2,1)} %reshape.513), calls=%async_computation.2 | async-start | bytes 65536 | tf_op jit(solution)/shard_map/all_to_all | solution.py:239
  167.4 2.0 convolution_dynamic-update-slice_fusion.7
  169.4 2.0 convolution_dynamic-update-slice_fusion.6
  180.0 2.2 collective-permute-start.9
  182.2 3.6 collective-permute-start.8
  185.8 6.3 %multiply_bitcast_fusion = f32[864,2,8,128]{3,2,1,0:T(8,128)} fusion(f32[6912,256]{1,0:T(8,128)} %convolution_dynamic-update-slice_fusion), kind=kLoop, calls=%fused_computation.1 | loop fusion | flops 1769472 | bytes 14155776
  192.1 9.5 %copy.256 = f32[864,2,8,128]{3,1,2,0:T(2,128)} copy(f32[864,2,8,128]{3,2,1,0:T(8,128)} %multiply_bitcast_fusion) | data formatting | bytes 14155776
  211.8 9.8 %all-to-all-start.4 = ((bf16[32,2,256]{2,1,0:T(2,128)(2,1)}), bf16[32,2,256]{2,1,0:T(2,128)(2,1)}, u32[]{:S(2)}, u32[]{:S(2)}) async-start(bf16[32,2,256]{2,1,0:T(2,128)(2,1)} %reshape.548), calls=%async_computation.4 | async-start | bytes 65536 | tf_op jit(solution)/shard_map/all_to_all | solution.py:239
  221.9 1.4 reshape.514
  225.0 1.7 dot_general.290
  226.8 3.3 add_convert_fusion
  234.1 4.8 multiply_convert_fusion
  248.2 7.5 %pad_maximum_fusion = f32[2060288]{0:T(1024)} fusion(f32[131072]{0:T(1024)S(1)} %bitcast.427, f32[1769472]{0:T(1024)} %bitcast.425, f32[131072]{0:T(1024)} %bitcast.428, f32[28672]{0:T(1024)S(1)} %div.64), kind=kLoop, calls=%fused_computation | loop fusion | flops 6180864 | bytes 16482304 | tf_op jit(solution)/shard_map/concatenate | solution.py:373
  255.8 3.4 collective-permute-start.10
  259.1 2.7 collective-permute-start.11
  263.1 1.5 fusion.217
  265.1 1.6 fusion.216
  266.6 2.4 reshape.550
  269.0 2.1 convolution_convert_fusion
  271.1 2.9 reshape.551
  274.1 3.1 fusion.15
  277.2 2.8 fusion.17
  280.0 3.1 fusion.19
  283.1 3.3 fusion.18
  286.4 2.8 fusion.16
  289.2 6.6 %fusion = bf16[12,64,512]{2,1,0:T(8,128)(2,1)} fusion(f32[12,64,512]{2,1,0:T(8,128)} %get-tuple-element.93, f32[12,512,64]{1,2,0:T(8,128)} %fusion.15, f32[12,512,64]{1,2,0:T(8,128)} %fusion.16, f32[12,512,64]{1,2,0:T(8,128)} %fusion.17, f32[12,512,64]{1,2,0:T(8,128)} %fusion.18, f32[12,512,64]{1,2,0:T(8,128)S(1)} %fusion.118, f32[12,512,64]{1,2,0:T(8,128)} %fusion.19, ...), kind=kOutput, calls=%fused_computation.7 | convolution fusion | flops 104595456 | bytes 12861952 | tf_op jit(solution)/shard_map/bov,ko->bkv/dot_general | solution.py:213
  295.8 237.3 %all-reduce.17.cloned.1.call-done = f32[2060288]{0:T(1024)} async-done(((f32[2060288]{0:T(1024)}), f32[2060288]{0:T(1024)}) %all-reduce.17.cloned.1.call-update) | async-done | bytes 8241168
  533.0 1.5 dynamic-slice
  (378 shorter events, 81.7 us)
Async XLA Ops:
  7.2 74.1 %copy-start = (bf16[256,512]{1,0:T(8,128)(2,1)S(1)}, bf16[256,512]{1,0:T(8,128)(2,1)}, u32[]{:S(2)}) copy-start(bf16[256,512]{1,0:T(8,128)(2,1)} %param.47) | copy-start | bytes 786436
  9.5 71.8 %copy-start.100 = (s32[12]{0:T(128)}, s32[12]{0:T(128)S(1)}, u32[]{:S(2)}) copy-start(s32[12]{0:T(128)S(1)} %get-tuple-element.96) | copy-start | bytes 148
  10.3 59.9 %all-to-all-start = ((s32[32,1,2]{2,1,0:T(1,128)}), s32[32,1,2]{2,1,0:T(1,128)}, u32[]{:S(2)}, u32[]{:S(2)}) async-start(s32[32,1,2]{2,1,0:T(1,128)} %bitcast.33), calls=%async_computation | async-start | bytes 32768 | tf_op jit(solution)/shard_map/all_to_all | solution.py:309
  28.3 7.9 %copy-start.2 = (bf16[12,64,512]{2,1,0:T(8,128)(2,1)S(1)}, bf16[12,64,512]{2,1,0:T(8,128)(2,1)}, u32[]{:S(2)}) copy-start(bf16[12,64,512]{2,1,0:T(8,128)(2,1)} %param.42) | copy-start | bytes 2359300
  30.0 15.7 %collective-permute-start = (bf16[1,6,4096]{2,1,0:T(8,128)(2,1)S(1)}, bf16[1,6,4096]{2,1,0:T(8,128)(2,1)S(1)}, u32[]{:S(2)}, u32[]{:S(2)}) collective-permute-start(bf16[1,6,4096]{2,1,0:T(8,128)(2,1)S(1)} %get-tuple-element.36), channel_id=1, source_target_pairs={{0,1},{1,2},{2,3},{3,4},{4,5},{5,6},{6,7},{7,8},{8,9},{9,10},{10,1... | collective-permute-start | bytes 147464 | tf_op jit(solution)/shard_map/ppermute | solution.py:24
  33.4 12.3 %collective-permute-start.1 = (bf16[1,6,4096]{2,1,0:T(8,128)(2,1)S(1)}, bf16[1,6,4096]{2,1,0:T(8,128)(2,1)}, u32[]{:S(2)}, u32[]{:S(2)}) collective-permute-start(bf16[1,6,4096]{2,1,0:T(8,128)(2,1)S(1)} %get-tuple-element.37), channel_id=1, source_target_pairs={{1,0},{2,1},{3,2},{4,3},{5,4},{6,5},{7,6},{8,7},{9,8},{10,9},{11,1... | collective-permute-start | bytes 147464 | tf_op jit(solution)/shard_map/ppermute | solution.py:26
  70.2 19.9 %all-to-all-start.1 = ((bf16[32,2,256]{2,1,0:T(2,128)(2,1)}), bf16[32,2,256]{2,1,0:T(2,128)(2,1)}, u32[]{:S(2)}, u32[]{:S(2)}) async-start(bf16[32,2,256]{2,1,0:T(2,128)(2,1)} %reshape.500), calls=%async_computation.1 | async-start | bytes 65536 | tf_op jit(solution)/shard_map/all_to_all | solution.py:239
  87.6 11.3 %copy-start.92 = (s32[64]{0:T(128)}, s32[64]{0:T(128)S(1)}, u32[]{:S(2)}) copy-start(s32[64]{0:T(128)S(1)} %eq.177) | copy-start | bytes 772
  90.1 35.6 %all-to-all-start.3 = ((bf16[32,2,256]{2,1,0:T(2,128)(2,1)}), bf16[32,2,256]{2,1,0:T(2,128)(2,1)}, u32[]{:S(2)}, u32[]{:S(2)}) async-start(bf16[32,2,256]{2,1,0:T(2,128)(2,1)} %reshape.516), calls=%async_computation.3 | async-start | bytes 65536 | tf_op jit(solution)/shard_map/all_to_all | solution.py:239
  99.8 27.4 %collective-permute-start.3 = (bf16[1,1,16,256]{3,2,1,0:T(8,128)(2,1)S(1)}, bf16[1,1,16,256]{3,2,1,0:T(8,128)(2,1)S(1)}, u32[]{:S(2)}, u32[]{:S(2)}) collective-permute-start(bf16[1,1,16,256]{3,2,1,0:T(8,128)(2,1)S(1)} %fusion.27), channel_id=1, source_target_pairs={{32,0},{64,32},{96,64},{128,96},{160,128},{192,160},{224,192},{33,... | collective-permute-start | bytes 24584 | tf_op jit(solution)/shard_map/ppermute | solution.py:26
  101.1 26.1 %collective-permute-start.2 = (bf16[1,1,16,256]{3,2,1,0:T(8,128)(2,1)S(1)}, bf16[1,1,16,256]{3,2,1,0:T(8,128)(2,1)}, u32[]{:S(2)}, u32[]{:S(2)}) collective-permute-start(bf16[1,1,16,256]{3,2,1,0:T(8,128)(2,1)S(1)} %fusion.27), channel_id=1, source_target_pairs={{0,32},{32,64},{64,96},{96,128},{128,160},{160,192},{192,224},{1,3... | collective-permute-start | bytes 24584 | tf_op jit(solution)/shard_map/ppermute | solution.py:24
  127.2 18.1 %copy-start.49 = (bf16[1,1,16,256]{3,2,1,0:T(8,128)(2,1)}, bf16[1,1,16,256]{3,2,1,0:T(8,128)(2,1)S(1)}, u32[]{:S(2)}) copy-start(bf16[1,1,16,256]{3,2,1,0:T(8,128)(2,1)S(1)} %collective-permute-done.3) | copy-start | bytes 24580
  127.9 7.3 %collective-permute-start.5 = (bf16[3,1,16,256]{3,2,1,0:T(8,128)(2,1)S(1)}, bf16[3,1,16,256]{3,2,1,0:T(8,128)(2,1)S(1)}, u32[]{:S(2)}, u32[]{:S(2)}) collective-permute-start(bf16[3,1,16,256]{3,2,1,0:T(8,128)(2,1)S(1)} %pad_maximum_fusion.1), channel_id=1, source_target_pairs={{1,0},{2,1},{3,2},{4,3},{5,4},{6,5},{7,6},{8,7},{9,8},{10,9},{11,1... | collective-permute-start | bytes 73736 | tf_op jit(solution)/shard_map/ppermute | solution.py:26
  130.1 5.7 %collective-permute-start.4 = (bf16[3,1,16,256]{3,2,1,0:T(8,128)(2,1)S(1)}, bf16[3,1,16,256]{3,2,1,0:T(8,128)(2,1)S(1)}, u32[]{:S(2)}, u32[]{:S(2)}) collective-permute-start(bf16[3,1,16,256]{3,2,1,0:T(8,128)(2,1)S(1)} %pad_maximum_fusion.1), channel_id=1, source_target_pairs={{0,1},{1,2},{2,3},{3,4},{4,5},{5,6},{6,7},{7,8},{8,9},{9,10},{10,1... | collective-permute-start | bytes 73736 | tf_op jit(solution)/shard_map/ppermute | solution.py:24
  135.1 11.3 %copy-start.51 = (f32[1,1,16,256]{3,2,1,0:T(8,128)}, f32[1,1,16,256]{3,2,1,0:T(8,128)S(1)}, u32[]{:S(2)}) copy-start(f32[1,1,16,256]{3,2,1,0:T(8,128)S(1)} %fusion.23) | copy-start | bytes 49156
  136.6 8.5 %copy-start.61 = (bf16[1,1,16,256]{3,2,1,0:T(8,128)(2,1)}, bf16[1,1,16,256]{3,2,1,0:T(8,128)(2,1)S(1)}, u32[]{:S(2)}) copy-start(bf16[1,1,16,256]{3,2,1,0:T(8,128)(2,1)S(1)} %get-tuple-element.59) | copy-start | bytes 24580
  136.6 8.5 %copy-start.63 = (bf16[1,1,16,256]{3,2,1,0:T(8,128)(2,1)}, bf16[1,1,16,256]{3,2,1,0:T(8,128)(2,1)S(1)}, u32[]{:S(2)}) copy-start(bf16[1,1,16,256]{3,2,1,0:T(8,128)(2,1)S(1)} %get-tuple-element.60) | copy-start | bytes 24580
  136.6 8.5 %copy-start.65 = (bf16[1,1,16,256]{3,2,1,0:T(8,128)(2,1)}, bf16[1,1,16,256]{3,2,1,0:T(8,128)(2,1)S(1)}, u32[]{:S(2)}) copy-start(bf16[1,1,16,256]{3,2,1,0:T(8,128)(2,1)S(1)} %get-tuple-element.61) | copy-start | bytes 24580
  136.6 8.5 %copy-start.67 = (bf16[1,1,16,256]{3,2,1,0:T(8,128)(2,1)}, bf16[1,1,16,256]{3,2,1,0:T(8,128)(2,1)S(1)}, u32[]{:S(2)}) copy-start(bf16[1,1,16,256]{3,2,1,0:T(8,128)(2,1)S(1)} %get-tuple-element.62) | copy-start | bytes 24580
  136.6 8.5 %copy-start.69 = (bf16[1,1,16,256]{3,2,1,0:T(8,128)(2,1)}, bf16[1,1,16,256]{3,2,1,0:T(8,128)(2,1)S(1)}, u32[]{:S(2)}) copy-start(bf16[1,1,16,256]{3,2,1,0:T(8,128)(2,1)S(1)} %get-tuple-element.63) | copy-start | bytes 24580
  136.6 8.5 %copy-start.71 = (bf16[1,1,16,256]{3,2,1,0:T(8,128)(2,1)}, bf16[1,1,16,256]{3,2,1,0:T(8,128)(2,1)S(1)}, u32[]{:S(2)}) copy-start(bf16[1,1,16,256]{3,2,1,0:T(8,128)(2,1)S(1)} %get-tuple-element.64) | copy-start | bytes 24580
  136.6 8.5 %copy-start.73 = (bf16[1,1,16,256]{3,2,1,0:T(8,128)(2,1)}, bf16[1,1,16,256]{3,2,1,0:T(8,128)(2,1)S(1)}, u32[]{:S(2)}) copy-start(bf16[1,1,16,256]{3,2,1,0:T(8,128)(2,1)S(1)} %get-tuple-element.65) | copy-start | bytes 24580
  136.7 8.5 %copy-start.75 = (bf16[1,1,16,256]{3,2,1,0:T(8,128)(2,1)}, bf16[1,1,16,256]{3,2,1,0:T(8,128)(2,1)S(1)}, u32[]{:S(2)}) copy-start(bf16[1,1,16,256]{3,2,1,0:T(8,128)(2,1)S(1)} %get-tuple-element.66) | copy-start | bytes 24580
  136.7 8.5 %copy-start.77 = (bf16[1,1,16,256]{3,2,1,0:T(8,128)(2,1)}, bf16[1,1,16,256]{3,2,1,0:T(8,128)(2,1)S(1)}, u32[]{:S(2)}) copy-start(bf16[1,1,16,256]{3,2,1,0:T(8,128)(2,1)S(1)} %get-tuple-element.67) | copy-start | bytes 24580
  136.7 8.5 %copy-start.78 = (bf16[1,1,16,256]{3,2,1,0:T(8,128)(2,1)}, bf16[1,1,16,256]{3,2,1,0:T(8,128)(2,1)S(1)}, u32[]{:S(2)}) copy-start(bf16[1,1,16,256]{3,2,1,0:T(8,128)(2,1)S(1)} %get-tuple-element.68) | copy-start | bytes 24580
  136.7 8.5 %copy-start.79 = (bf16[1,1,16,256]{3,2,1,0:T(8,128)(2,1)}, bf16[1,1,16,256]{3,2,1,0:T(8,128)(2,1)S(1)}, u32[]{:S(2)}) copy-start(bf16[1,1,16,256]{3,2,1,0:T(8,128)(2,1)S(1)} %get-tuple-element.69) | copy-start | bytes 24580
  136.7 8.5 %copy-start.80 = (bf16[1,1,16,256]{3,2,1,0:T(8,128)(2,1)}, bf16[1,1,16,256]{3,2,1,0:T(8,128)(2,1)S(1)}, u32[]{:S(2)}) copy-start(bf16[1,1,16,256]{3,2,1,0:T(8,128)(2,1)S(1)} %get-tuple-element.70) | copy-start | bytes 24580
  136.7 8.5 %copy-start.57 = (bf16[1,1,16,256]{3,2,1,0:T(8,128)(2,1)}, bf16[1,1,16,256]{3,2,1,0:T(8,128)(2,1)S(1)}, u32[]{:S(2)}) copy-start(bf16[1,1,16,256]{3,2,1,0:T(8,128)(2,1)S(1)} %get-tuple-element.57) | copy-start | bytes 24580
  136.7 8.5 %copy-start.59 = (bf16[1,1,16,256]{3,2,1,0:T(8,128)(2,1)}, bf16[1,1,16,256]{3,2,1,0:T(8,128)(2,1)S(1)}, u32[]{:S(2)}) copy-start(bf16[1,1,16,256]{3,2,1,0:T(8,128)(2,1)S(1)} %get-tuple-element.58) | copy-start | bytes 24580
  136.7 9.7 %copy-start.53 = (bf16[1,1,16,256]{3,2,1,0:T(8,128)(2,1)}, bf16[1,1,16,256]{3,2,1,0:T(8,128)(2,1)S(1)}, u32[]{:S(2)}) copy-start(bf16[1,1,16,256]{3,2,1,0:T(8,128)(2,1)S(1)} %get-tuple-element.56) | copy-start | bytes 24580
  136.7 9.7 %copy-start.55 = (bf16[1,1,16,256]{3,2,1,0:T(8,128)(2,1)}, bf16[1,1,16,256]{3,2,1,0:T(8,128)(2,1)S(1)}, u32[]{:S(2)}) copy-start(bf16[1,1,16,256]{3,2,1,0:T(8,128)(2,1)S(1)} %get-tuple-element.73) | copy-start | bytes 24580
  136.8 8.4 %copy-start.84 = (bf16[1,1,16,256]{3,2,1,0:T(8,128)(2,1)}, bf16[1,1,16,256]{3,2,1,0:T(8,128)(2,1)S(1)}, u32[]{:S(2)}) copy-start(bf16[1,1,16,256]{3,2,1,0:T(8,128)(2,1)S(1)} %get-tuple-element.83) | copy-start | bytes 24580
  136.8 8.4 %copy-start.88 = (bf16[1,1,16,256]{3,2,1,0:T(8,128)(2,1)}, bf16[1,1,16,256]{3,2,1,0:T(8,128)(2,1)S(1)}, u32[]{:S(2)}) copy-start(bf16[1,1,16,256]{3,2,1,0:T(8,128)(2,1)S(1)} %get-tuple-element.84) | copy-start | bytes 24580
  137.9 8.5 %copy-start.86 = (bf16[1,1,16,256]{3,2,1,0:T(8,128)(2,1)}, bf16[1,1,16,256]{3,2,1,0:T(8,128)(2,1)S(1)}, u32[]{:S(2)}) copy-start(bf16[1,1,16,256]{3,2,1,0:T(8,128)(2,1)S(1)} %get-tuple-element.81) | copy-start | bytes 24580
  138.0 8.5 %copy-start.90 = (bf16[1,1,16,256]{3,2,1,0:T(8,128)(2,1)}, bf16[1,1,16,256]{3,2,1,0:T(8,128)(2,1)S(1)}, u32[]{:S(2)}) copy-start(bf16[1,1,16,256]{3,2,1,0:T(8,128)(2,1)S(1)} %get-tuple-element.82) | copy-start | bytes 24580
  138.0 8.5 %copy-start.82 = (bf16[1,1,16,256]{3,2,1,0:T(8,128)(2,1)}, bf16[1,1,16,256]{3,2,1,0:T(8,128)(2,1)S(1)}, u32[]{:S(2)}) copy-start(bf16[1,1,16,256]{3,2,1,0:T(8,128)(2,1)S(1)} %get-tuple-element.80) | copy-start | bytes 24580
  141.5 12.3 %copy-start.93 = (s32[64]{0:T(128)S(1)}, s32[64]{0:T(128)}, u32[]{:S(2)}) copy-start(s32[64]{0:T(128)} %copy-done.92) | copy-start | bytes 772
  147.7 6.1 %copy-start.99 = (bf16[1,1,16,256]{3,2,1,0:T(8,128)(2,1)}, bf16[1,1,16,256]{3,2,1,0:T(8,128)(2,1)S(1)}, u32[]{:S(2)}) copy-start(bf16[1,1,16,256]{3,2,1,0:T(8,128)(2,1)S(1)} %get-tuple-element.87) | copy-start | bytes 24580
  147.7 30.9 %collective-permute-start.7 = (bf16[1,1,16,256]{3,2,1,0:T(8,128)(2,1)S(1)}, bf16[1,1,16,256]{3,2,1,0:T(8,128)(2,1)}, u32[]{:S(2)}, u32[]{:S(2)}) collective-permute-start(bf16[1,1,16,256]{3,2,1,0:T(8,128)(2,1)S(1)} %get-tuple-element.86), channel_id=1, source_target_pairs={{32,0},{64,32},{96,64},{128,96},{160,128},{192,160},{224,192},{33,... | collective-permute-start | bytes 24584 | tf_op jit(solution)/shard_map/ppermute | solution.py:26
  149.0 29.6 %collective-permute-start.6 = (bf16[1,1,16,256]{3,2,1,0:T(8,128)(2,1)S(1)}, bf16[1,1,16,256]{3,2,1,0:T(8,128)(2,1)}, u32[]{:S(2)}, u32[]{:S(2)}) collective-permute-start(bf16[1,1,16,256]{3,2,1,0:T(8,128)(2,1)S(1)} %get-tuple-element.86), channel_id=1, source_target_pairs={{0,32},{32,64},{64,96},{96,128},{128,160},{160,192},{192,224},{1,3... | collective-permute-start | bytes 24584 | tf_op jit(solution)/shard_map/ppermute | solution.py:24
  156.0 55.8 %all-to-all-start.2 = ((bf16[32,2,256]{2,1,0:T(2,128)(2,1)}), bf16[32,2,256]{2,1,0:T(2,128)(2,1)}, u32[]{:S(2)}, u32[]{:S(2)}) async-start(bf16[32,2,256]{2,1,0:T(2,128)(2,1)} %reshape.513), calls=%async_computation.2 | async-start | bytes 65536 | tf_op jit(solution)/shard_map/all_to_all | solution.py:239
  167.4 5.2 copy-start.70
  167.4 5.2 copy-start.72
  167.4 6.4 %copy-start.66 = (bf16[1,1,16,256]{3,2,1,0:T(8,128)(2,1)S(1)}, bf16[1,1,16,256]{3,2,1,0:T(8,128)(2,1)}, u32[]{:S(2)}) copy-start(bf16[1,1,16,256]{3,2,1,0:T(8,128)(2,1)} %copy-done.65) | copy-start | bytes 24580
  167.4 6.4 %copy-start.68 = (bf16[1,1,16,256]{3,2,1,0:T(8,128)(2,1)S(1)}, bf16[1,1,16,256]{3,2,1,0:T(8,128)(2,1)}, u32[]{:S(2)}) copy-start(bf16[1,1,16,256]{3,2,1,0:T(8,128)(2,1)} %copy-done.67) | copy-start | bytes 24580
  167.4 6.4 %copy-start.87 = (bf16[1,1,16,256]{3,2,1,0:T(8,128)(2,1)S(1)}, bf16[1,1,16,256]{3,2,1,0:T(8,128)(2,1)}, u32[]{:S(2)}) copy-start(bf16[1,1,16,256]{3,2,1,0:T(8,128)(2,1)} %copy-done.86) | copy-start | bytes 24580
  169.4 5.6 %copy-start.62 = (bf16[1,1,16,256]{3,2,1,0:T(8,128)(2,1)S(1)}, bf16[1,1,16,256]{3,2,1,0:T(8,128)(2,1)}, u32[]{:S(2)}) copy-start(bf16[1,1,16,256]{3,2,1,0:T(8,128)(2,1)} %copy-done.61) | copy-start | bytes 24580
  169.4 5.6 %copy-start.64 = (bf16[1,1,16,256]{3,2,1,0:T(8,128)(2,1)S(1)}, bf16[1,1,16,256]{3,2,1,0:T(8,128)(2,1)}, u32[]{:S(2)}) copy-start(bf16[1,1,16,256]{3,2,1,0:T(8,128)(2,1)} %copy-done.63) | copy-start | bytes 24580
  169.4 5.6 %copy-start.85 = (bf16[1,1,16,256]{3,2,1,0:T(8,128)(2,1)S(1)}, bf16[1,1,16,256]{3,2,1,0:T(8,128)(2,1)}, u32[]{:S(2)}) copy-start(bf16[1,1,16,256]{3,2,1,0:T(8,128)(2,1)} %copy-done.84) | copy-start | bytes 24580
  180.0 21.7 %collective-permute-start.9 = (bf16[3,1,16,256]{3,2,1,0:T(8,128)(2,1)}, bf16[3,1,16,256]{3,2,1,0:T(8,128)(2,1)}, u32[]{:S(2)}, u32[]{:S(2)}) collective-permute-start(bf16[3,1,16,256]{3,2,1,0:T(8,128)(2,1)} %pad_maximum_fusion.2), channel_id=1, source_target_pairs={{1,0},{2,1},{3,2},{4,3},{5,4},{6,5},{7,6},{8,7},{9,8},{10,9},{11,1... | collective-permute-start | bytes 73736 | tf_op jit(solution)/shard_map/ppermute | solution.py:26
  182.2 19.5 %collective-permute-start.8 = (bf16[3,1,16,256]{3,2,1,0:T(8,128)(2,1)}, bf16[3,1,16,256]{3,2,1,0:T(8,128)(2,1)}, u32[]{:S(2)}, u32[]{:S(2)}) collective-permute-start(bf16[3,1,16,256]{3,2,1,0:T(8,128)(2,1)} %pad_maximum_fusion.2), channel_id=1, source_target_pairs={{0,1},{1,2},{2,3},{3,4},{4,5},{5,6},{6,7},{7,8},{8,9},{9,10},{10,1... | collective-permute-start | bytes 73736 | tf_op jit(solution)/shard_map/ppermute | solution.py:24
  201.6 6.1 %copy-start.27 = (bf16[3,256,256]{2,1,0:T(8,128)(2,1)S(1)}, bf16[3,256,256]{2,1,0:T(8,128)(2,1)}, u32[]{:S(2)}) copy-start(bf16[3,256,256]{2,1,0:T(8,128)(2,1)} %copy.204) | copy-start | bytes 1179652
  201.6 6.3 %copy-start.26 = (bf16[3,256,256]{2,1,0:T(8,128)(2,1)S(1)}, bf16[3,256,256]{2,1,0:T(8,128)(2,1)}, u32[]{:S(2)}) copy-start(bf16[3,256,256]{2,1,0:T(8,128)(2,1)} %copy.205) | copy-start | bytes 1179652
  201.6 6.5 %copy-start.24 = (bf16[3,256,256]{2,1,0:T(8,128)(2,1)S(1)}, bf16[3,256,256]{2,1,0:T(8,128)(2,1)}, u32[]{:S(2)}) copy-start(bf16[3,256,256]{2,1,0:T(8,128)(2,1)} %copy.206) | copy-start | bytes 1179652
  202.6 5.8 %copy-start.23 = (bf16[3,256,256]{2,1,0:T(8,128)(2,1)S(1)}, bf16[3,256,256]{2,1,0:T(8,128)(2,1)}, u32[]{:S(2)}) copy-start(bf16[3,256,256]{2,1,0:T(8,128)(2,1)} %copy.207) | copy-start | bytes 1179652
  203.4 5.1 copy-start.25
  209.6 21.4 %copy-start.81 = (bf16[1,1,16,256]{3,2,1,0:T(8,128)(2,1)}, bf16[1,1,16,256]{3,2,1,0:T(8,128)(2,1)S(1)}, u32[]{:S(2)}) copy-start(bf16[1,1,16,256]{3,2,1,0:T(8,128)(2,1)S(1)} %fusion.29) | copy-start | bytes 24580
  211.8 20.1 %all-to-all-start.4 = ((bf16[32,2,256]{2,1,0:T(2,128)(2,1)}), bf16[32,2,256]{2,1,0:T(2,128)(2,1)}, u32[]{:S(2)}, u32[]{:S(2)}) async-start(bf16[32,2,256]{2,1,0:T(2,128)(2,1)} %reshape.548), calls=%async_computation.4 | async-start | bytes 65536 | tf_op jit(solution)/shard_map/all_to_all | solution.py:239
  221.7 311.3 %all-reduce.17.cloned.1.call-start = ((), (), s32[]{:S(2)}) async-start(), calls=%async_computation.5 | async-start | bytes 16482304
  226.8 6.2 %copy-start.28 = (bf16[512,256]{1,0:T(8,128)(2,1)S(1)}, bf16[512,256]{1,0:T(8,128)(2,1)}, u32[]{:S(2)}) copy-start(bf16[512,256]{1,0:T(8,128)(2,1)} %param.45) | copy-start | bytes 786436
  246.7 9.0 %copy-start.12 = (bf16[12,6,64,64]{3,2,1,0:T(8,128)(2,1)}, bf16[12,6,64,64]{3,2,1,0:T(8,128)(2,1)S(1)}, u32[]{:S(2)}) copy-start(bf16[12,6,64,64]{3,2,1,0:T(8,128)(2,1)S(1)} %fusion.2) | copy-start | bytes 1769476
  255.8 13.2 %collective-permute-start.10 = (bf16[1,6,4096]{2,1,0:T(8,128)(2,1)S(1)}, bf16[1,6,4096]{2,1,0:T(8,128)(2,1)S(1)}, u32[]{:S(2)}, u32[]{:S(2)}) collective-permute-start(bf16[1,6,4096]{2,1,0:T(8,128)(2,1)S(1)} %get-tuple-element.34), channel_id=1, source_target_pairs={{0,1},{1,2},{2,3},{3,4},{4,5},{5,6},{6,7},{7,8},{8,9},{9,10},{10,1... | collective-permute-start | bytes 147464 | tf_op jit(solution)/shard_map/ppermute | solution.py:24
  259.1 9.9 %collective-permute-start.11 = (bf16[1,6,4096]{2,1,0:T(8,128)(2,1)S(1)}, bf16[1,6,4096]{2,1,0:T(8,128)(2,1)}, u32[]{:S(2)}, u32[]{:S(2)}) collective-permute-start(bf16[1,6,4096]{2,1,0:T(8,128)(2,1)S(1)} %get-tuple-element.35), channel_id=1, source_target_pairs={{1,0},{2,1},{3,2},{4,3},{5,4},{6,5},{7,6},{8,7},{9,8},{10,9},{11,1... | collective-permute-start | bytes 147464 | tf_op jit(solution)/shard_map/ppermute | solution.py:26
  289.2 245.3 %copy-start.1 = (bf16[256,512]{1,0:T(8,128)(2,1)S(1)}, bf16[256,512]{1,0:T(8,128)(2,1)}, u32[]{:S(2)}) copy-start(bf16[256,512]{1,0:T(8,128)(2,1)} %param.47) | copy-start | bytes 786436
  (73 other events, 177.3 us)
Sparse Core Ops, SparseCore 0:
  255.9 277.1 all-reduce.16
where the time goes:
time: 551 us; the launch traced here: 542 us
  waiting for transfers between devices  240 us (44%)
  matrix products  91.3 us (17%)
  local copies, waits for them, and re-layouts  85.4 us (15%)
  starting transfers between devices  85.2 us (15%)
  other arithmetic  23.3 us (4%)
  between operations  15.9 us (3%)
    unnamed x2, waiting for transfers between devices  237 us
    all_to_all x4, starting transfers between devices, swap_rows(): lax.all_to_all(packed, 'blk', split_axis=0, concat_axis=0, tiled=True)  39.5 us
    ppermute x6, starting transfers between devices, extended_2(): lax.ppermute(tail, axis, [(i, (i + 1) % count) for i in range(ends)])  21.8 us
    dot_general x6, matrix products, fine_transpose(): jnp.einsum('bov,ko->bkv', back_list[OPPOSITE[direction]], block_w, prefer...  21.6 us
    unnamed x242, local copies, waits for them, and re-layouts  20.3 us
    transpose x9, local copies, waits for them, and re-layouts, coarse_transpose(): block_w = weight[offset:offset + 3 * width_c].reshape(3, width_c, width_c...  17.3 us
    ppermute x6, starting transfers between devices, extended_2(): lax.ppermute(head, axis, [((i + 1) % count, i) for i in range(ends)])  12.4 us
    dot_general x9, matrix products, coarse_weight_grad(): lax.dot_general(joined, flat_grad, (((0,), (0,)), ((), ())), preferred_el...  12.3 us
  transfers between devices with their start and end apart: 18, of which 3 were waited for; matrix products, arithmetic and copies ran while one was open for 28% of the time, Pallas kernels for 0%

commit v1 on v0

v1 whole, which is shorter than its diff:
```python
import functools
import math

import jax
import jax.numpy as jnp
import numpy as np
from jax import lax
from jax.experimental import pallas as pl
from jax.experimental.pallas import tpu as pltpu
from jax.sharding import PartitionSpec as P

NB = 12
CH = 64
VOX = 512
WID = 256
CELLS = 16
FB = 6
OPPOSITE = (1, 0, 3, 2, 5, 4)
STRIDES = (64, 8, 1)
FACES = NB * 6
PREV0 = FACES
NEXT0 = FACES + 3
ZERO = FACES + 6
SLOTS = FACES + 7
OFFSETS = ((-1, -1), (-1, 0), (-1, 1), (0, -1), (0, 1), (1, -1), (1, 0), (1, 1))
SHARD = 8048
SLAB_ROWS = 1006
MESH = pl.DeviceIdType.MESH
F32 = jnp.float32
BF16 = jnp.bfloat16


def tables():
    voxel = np.arange(VOX)
    coords = (voxel // 64, voxel // 8 % 8, voxel % 8)
    octant = 4 * (coords[0] // 4) + 2 * (coords[1] // 4) + coords[2] // 4
    pull = np.zeros((VOX, 6 * 128), np.float32)
    place = np.zeros((6, 128, VOX), np.float32)
    keep = np.ones((6, 1, VOX), np.float32)
    for axis in range(3):
        others = [coords[other] for other in range(3) if other != axis]
        index = others[0] * 8 + others[1]
        for side in range(2):
            d = 2 * axis + side
            on = coords[axis] == 7 * side
            keep[d, 0, on] = 0.0
            for half in range(2):
                pull[voxel[on], 128 * d + 64 * half + index[on]] = 1.0
                place[d, 64 * half + index[on], voxel[on]] = 1.0
    spread = (octant[:, None] == np.arange(VOX)[None, :] // 64).astype(np.float32)
    major = np.arange(VOX)
    perm = np.zeros((VOX, VOX), np.float32)
    perm[major, 8 * (major % 64) + major // 64] = 1.0
    bf = lambda a: jnp.asarray(a, BF16)
    return bf(pull), bf(place), jnp.asarray(keep), bf(spread), bf(spread.T), bf(perm), bf(perm.T)


def dot(a, b):
    return jnp.dot(a, b, preferred_element_type=F32)


def dot_nt(a, b):
    return lax.dot_general(a, b, (((1,), (1,)), ((), ())), preferred_element_type=F32)


def dot_tn(a, b):
    return lax.dot_general(a, b, (((0,), (0,)), ((), ())), preferred_element_type=F32)


def iota(shape, dim):
    return lax.broadcasted_iota(jnp.int32, shape, dim)


def kernel(
    n_slab, n_blk,
    fine, cot, latent, cotc, w_fine, w_down, w_up, w_coarse_hbm, send_sm, code_sm, owner, cell,
    pull, place, keep, spread, spread_t, perm, perm_t,
    fine_out, coarse_out, grad_fine, grad_latent, grads_out,
    w_coarse, faces1, faces2, pack1, pack2, near, placed, taps, pre, mid, dpf, big, ysum, yrow,
    wbig, pk, arr, rpk, rarr, rim1, rim2, rimsrc1, rimsrc2, gacc, land1, land2,
    gsrc, gat, xq, gbuf, wland, ssrc, sland, fsrc, fland, units, uland, gsum,
    wsem, fsend, frecv, asend, arecv, rsend, rrecv, gsend, grecv, vsend, vrecv, usend, urecv,
):
    me_s = lax.axis_index("slab")
    me_b = lax.axis_index("blk")
    total = n_slab * n_blk
    pos = me_s * n_blk + me_b
    after = lax.rem(pos + 1, total)
    before = lax.rem(pos + total - 1, total)
    rel = lambda i: (me_s, lax.rem(me_b + i, n_blk))
    column = lambda i: (lax.rem(me_s + i, n_slab), me_b)
    flat = lambda k: (lax.div(k, n_blk), lax.rem(k, n_blk))
    near_id = lambda a, b: (lax.rem(me_s + a + n_slab, n_slab), lax.rem(me_b + b + n_blk, n_blk))

    load_w = pltpu.make_async_copy(w_coarse_hbm, w_coarse, wsem)
    load_w.start()

    barrier = pltpu.get_barrier_semaphore()

    def greet(i, carry):
        pl.semaphore_signal(barrier, inc=1, device_id=rel(i), device_id_type=MESH)
        return carry

    lax.fori_loop(1, n_blk, greet, 0)
    for i in range(1, n_slab):
        pl.semaphore_signal(barrier, inc=1, device_id=column(i), device_id_type=MESH)
    for a, b in OFFSETS:
        if a != 0 and b != 0:
            pl.semaphore_signal(barrier, inc=1, device_id=near_id(a, b), device_id_type=MESH)
    for k in (before, after):
        pl.semaphore_signal(barrier, inc=1, device_id=flat(k), device_id_type=MESH)

    lane64 = iota((CH, 128), 1) // 64
    eye = (iota((CH, VOX), 1) % 64 == iota((CH, VOX), 0)).astype(F32)

    def make_faces(src, faces, pack):
        faces[ZERO] = jnp.zeros((CH, 128), BF16)

        def pull_group(g, carry):
            rows = src[pl.ds(g * 4, 4)].reshape(4 * CH, VOX)
            out = dot(rows, pull[...]).astype(BF16)
            for bb in range(4):
                for d in range(6):
                    faces[(g * 4 + bb) * 6 + d] = out[CH * bb : CH * bb + CH, 128 * d : 128 * d + 128]
            return carry

        lax.fori_loop(0, NB // 4, pull_group, 0)
        for s in range(2):
            for q in range(3):
                first = faces[send_sm[s * FB + 2 * q]].astype(F32)
                second = faces[send_sm[s * FB + 2 * q + 1]].astype(F32)
                pack[s, q] = jnp.where(lane64 == 0, first, second).astype(BF16)

    def face_copies(land, pack, k):
        return [
            pltpu.make_async_remote_copy(
                src_ref=pack.at[0], dst_ref=land.at[pl.ds(3, 3)],
                send_sem=fsend.at[2 * k], recv_sem=frecv.at[2 * k],
                device_id=flat(before), device_id_type=MESH,
            ),
            pltpu.make_async_remote_copy(
                src_ref=pack.at[1], dst_ref=land.at[pl.ds(0, 3)],
                send_sem=fsend.at[2 * k + 1], recv_sem=frecv.at[2 * k + 1],
                device_id=flat(after), device_id_type=MESH,
            ),
        ]

    def roll_taps(src):
        def body(b, carry):
            x = src[b]
            wide = x.astype(F32)
            taps[b, 0:CH, :] = x
            for d in range(6):
                stride = STRIDES[d // 2]
                moved = pltpu.roll(wide, stride if d % 2 == 0 else VOX - stride, 1)
                taps[b, CH * (d + 1) : CH * (d + 2), :] = (moved * keep[d]).astype(BF16)
            return carry

        lax.fori_loop(0, NB, body, 0)

    def place_faces(faces, land):
        faces[PREV0 : PREV0 + 6] = land[...]
        for d in range(6):
            def gather(b, carry):
                code = code_sm[b * 6 + d]
                x = faces[lax.shift_right_logical(code, 1)].astype(F32)
                near[b] = jnp.where(lane64 == lax.bitwise_and(code, 1), x, 0.0).astype(BF16)
                return carry

            lax.fori_loop(0, NB, gather, 0)

            def put(g, carry):
                rows = near[pl.ds(g * 4, 4)].reshape(4 * CH, 128)
                placed[d, pl.ds(g * 4, 4)] = dot(rows, place[d]).astype(BF16).reshape(4, CH, VOX)
                return carry

            lax.fori_loop(0, NB // 4, put, 0)

    def full_taps(b):
        for d in range(6):
            rows = pl.ds(CH * (d + 1), CH)
            taps[b, rows, :] = taps[b, rows, :] + placed[d, b]
        return taps[b]

    def octant_rows(src):
        for g in range(NB // 4):
            rows = src[4 * g : 4 * g + 4].reshape(4 * CH, VOX)
            sums = dot(rows, spread[...])
            for bb in range(4):
                part = sums[CH * bb : CH * bb + CH] * eye
                ysum[4 * g + bb : 4 * g + bb + 1, :] = jnp.sum(part, axis=0, keepdims=True)
        return ysum[...]

    def expand(g):
        parts = []
        for bb in range(4):
            row = yrow[pl.ds(4 * g + bb, 1), :]
            parts.append((row * eye).astype(BF16))
        return dot(jnp.concatenate(parts, axis=0), spread_t[...])

    make_faces(fine, faces1, pack1)
    pl.semaphore_wait(barrier, n_blk - 1 + n_slab - 1 + 4 + 2)
    copies1 = face_copies(land1, pack1, 0)
    for copy in copies1:
        copy.start()

    roll_taps(fine)
    ysum[...] = jnp.zeros((CELLS, VOX), F32)
    d_raised = dot(octant_rows(cot).astype(BF16), perm[...]).astype(BF16)
    d_lifted = dot_nt(d_raised, w_up[...]).astype(BF16)
    ident = (iota((CH, CH), 0) == iota((CH, CH), 1)).astype(BF16)
    w_fwd = dot_nt(ident, w_fine[...]).astype(BF16)
    for e in range(7):
        d = 0 if e == 0 else OPPOSITE[e - 1] + 1
        wbig[:, CH * e : CH * e + CH] = w_fine[CH * d : CH * d + CH, :].astype(F32)

    own_col = owner[...]
    cell_col = cell[...]
    eye16 = iota((CELLS, 128), 0) == iota((CELLS, 128), 1)
    own_row = jnp.sum(jnp.where(eye16, own_col, 0), axis=0, keepdims=True)
    same = (own_col == own_row) & (iota((CELLS, 128), 1) < iota((CELLS, 128), 0))
    slot = jnp.sum(same.astype(jnp.int32), axis=1, keepdims=True)
    ahead = lax.rem(own_col - me_b + n_blk, n_blk)
    start = jnp.where(iota((CELLS, 1), 0) < NB, ahead * 16 + 5 * slot, -1000)
    start_col = jnp.concatenate([start + j for j in range(5)] + [start * 0 - 1000] * 3, axis=0)
    packet_rows = n_blk * 16
    route_t = (iota((128, packet_rows), 1) == start_col).astype(BF16)
    eye128 = iota((128, 128), 0) == iota((128, 128), 1)
    start_row = jnp.sum(jnp.where(eye128, start_col, 0), axis=0, keepdims=True)
    route = (iota((packet_rows, 128), 0) == start_row).astype(BF16)
    cell_hot = ((iota((CELLS, 128), 1) == cell_col) & (iota((CELLS, 128), 0) < NB)).astype(F32)

    for copy in copies1:
        copy.wait_recv()
    place_faces(faces1, land1)

    def fine_forward(b, carry):
        value = dot(w_fwd, full_taps(b))
        pre[b] = value
        mid[b] = (fine[b].astype(F32) + value * jax.nn.sigmoid(value)).astype(BF16)
        return carry

    lax.fori_loop(0, NB, fine_forward, 0)
    means = dot((octant_rows(mid) * (1.0 / 64.0)).astype(BF16), perm[...]).astype(BF16)
    pooled = dot(means, w_down[...]).astype(BF16).astype(F32)
    lift32 = d_lifted.astype(F32)
    payload = jnp.concatenate(
        [pooled[:, :128], pooled[:, 128:], lift32[:, :128], lift32[:, 128:], cell_hot,
         jnp.zeros((48, 128), F32)], axis=0).astype(BF16)
    pk[...] = dot(route, payload).astype(BF16).reshape(n_blk, 16, 128)
    arr[0] = pk[0]

    def row_copy(src, dst, i, back, k):
        return pltpu.make_async_remote_copy(
            src_ref=src.at[i], dst_ref=dst.at[i], send_sem=asend.at[k], recv_sem=arecv.at[k],
            device_id=rel(n_blk - i if back else i), device_id_type=MESH,
        )

    def row_wait(buf, sem):
        pltpu.make_async_copy(buf.at[pl.ds(1, n_blk - 1)], buf.at[pl.ds(1, n_blk - 1)], sem).wait()

    def send_rows(src, dst, back, k):
        def body(i, carry):
            row_copy(src, dst, i, back, k).start()
            return carry

        lax.fori_loop(1, n_blk, body, 0)

    send_rows(pk, arr, False, 0)
    load_w.wait()
    row_wait(arr, arecv.at[0])

    arrived = arr[...].reshape(packet_rows, 128)
    wide = arrived.astype(F32)
    row_of = iota((packet_rows, 128), 0) % 16
    hot = jnp.where((row_of == 4) | (row_of == 9), wide, 0.0)
    hot_t = hot.T[:CELLS].astype(BF16)
    lined = jnp.concatenate([pltpu.roll(wide, 4 - j, 0) for j in range(4)], axis=1).astype(BF16)
    added = dot(hot_t, lined)
    hot16 = hot.astype(BF16)

    d_cout = cotc[...].astype(F32) + added[:, WID:]
    c_in = (latent[...].astype(F32) + added[:, :WID]).astype(BF16)

    def rim_copies(src, dst, k):
        return [
            pltpu.make_async_remote_copy(
                src_ref=src, dst_ref=dst.at[7 - i], send_sem=rsend.at[8 * k + i],
                recv_sem=rrecv.at[8 * k + 7 - i], device_id=near_id(a, b), device_id_type=MESH,
            )
            for i, (a, b) in enumerate(OFFSETS)
        ]

    def rim_tile(dst, own, a, b):
        if a == 0 and b == 0:
            return own.astype(F32)
        zz, yy = me_s + a, me_b + b
        inside = (zz >= 0) & (zz < n_slab) & (yy >= 0) & (yy < n_blk)
        tile = dst[OFFSETS.index((a, b))].astype(F32)
        return tile * jnp.where(inside, 1.0, 0.0)

    sub = iota((CELLS, WID), 0)

    def along_x(tile, step):
        if step == 0:
            return tile
        moved = pltpu.roll(tile, 1 if step == -1 else CELLS - 1, 0)
        return jnp.where(sub == (0 if step == -1 else CELLS - 1), 0.0, moved)

    rimsrc1[...] = c_in
    copies2 = rim_copies(rimsrc1, rim1, 0)
    for copy in copies2:
        copy.start()
    for copy in copies2:
        copy.wait_recv()
    acc = jnp.zeros((CELLS, WID), F32)
    for p in range(3):
        for q in range(3):
            tile = rim_tile(rim1, c_in, p - 1, q - 1)
            row = jnp.concatenate([along_x(tile, r - 1) for r in range(3)], axis=1).astype(BF16)
            base = (p * 3 + q) * 3 * WID
            acc = acc + dot(row, w_coarse[base : base + 3 * WID, :])
    sig = jax.nn.sigmoid(acc)
    c_out = (c_in.astype(F32) + acc * sig).astype(BF16)
    coarse_out[...] = c_out
    d_pre = (d_cout * (sig * (1.0 + acc * (1.0 - sig)))).astype(BF16)
    rimsrc2[...] = d_pre
    copies3 = rim_copies(rimsrc2, rim2, 1)
    for copy in copies3:
        copy.start()

    gsrc[...] = jnp.concatenate(
        [rim_tile(rim1, c_in, 0, q - 1) for q in range(3)] + [d_pre.astype(F32)], axis=1
    ).astype(BF16)
    own_gather = pltpu.make_async_copy(gsrc, gat.at[me_s], grecv)
    own_gather.start()
    gathers = [
        pltpu.make_async_remote_copy(
            src_ref=gsrc, dst_ref=gat.at[me_s], send_sem=gsend.at[i - 1], recv_sem=grecv,
            device_id=column(i), device_id_type=MESH,
        )
        for i in range(1, n_slab)
    ]
    for copy in gathers:
        copy.start()
    for copy in copies3:
        copy.wait_recv()
    acc = d_cout
    for p in range(3):
        for q in range(3):
            tile = rim_tile(rim2, d_pre, 1 - p, 1 - q)
            for r in range(3):
                base = ((p * 3 + q) * 3 + r) * WID
                moved = along_x(tile, 1 - r).astype(BF16)
                acc = acc + dot_nt(moved, w_coarse[base : base + WID, :])
    g_lat = acc.astype(BF16)
    grad_latent[...] = g_lat

    grid = jnp.concatenate([c_out.astype(F32), g_lat.astype(F32)], axis=1)
    grid = jnp.concatenate([grid, jnp.zeros((128 - CELLS, 2 * WID), F32)], axis=0).astype(BF16)
    picked = dot(hot16, grid)
    back = jnp.zeros((packet_rows, 128), F32)
    for j in range(4):
        back = back + pltpu.roll(picked[:, 128 * j : 128 * j + 128], packet_rows - 4 + j, 0)
    rpk[...] = back.astype(BF16).reshape(n_blk, 16, 128)
    rarr[0] = rpk[0]
    send_rows(rpk, rarr, True, 1)

    base_row = me_s * SLAB_ROWS + 144
    first_tap = base_row // WID - 3
    skew = base_row % WID
    pltpu.make_async_copy(gat, gat, grecv).wait()
    everything = gat[...].reshape(n_slab * CELLS, 4 * WID).astype(F32)
    for q in range(3):
        xq[q] = everything[:, q * WID : q * WID + WID].T.astype(BF16)
    d_all = everything[:, 3 * WID :].astype(BF16)
    from_row = iota((128, 128), 0)
    to_row = iota((128, 128), 1)

    def tap_rows(i, carry):
        t = first_tap + i
        inside = (t >= 0) & (t < 27)
        tc = jnp.clip(t, 0, 26)
        p, q, r = tc // 9, tc // 3 % 3, tc % 3
        shift = (from_row // 16 == to_row // 16 + p - 1) & (
            from_row % 16 == to_row % 16 + r - 1)
        moved = dot(xq[q], shift.astype(BF16)).astype(BF16)
        gbuf[pl.ds(pl.multiple_of(i * WID, WID), WID), :] = (
            dot(moved, d_all) * jnp.where(inside, 1.0 / math.sqrt(CELLS * total), 0.0)
        ).astype(BF16)
        return carry

    lax.fori_loop(0, 5, tap_rows, 0)

    def window_of(k):
        unit = (16 * skew + 503 * k) // 256
        return gbuf.at[pl.ds(pl.multiple_of(16 * unit, 16), 48)]

    def send_window(i, carry):
        pltpu.make_async_remote_copy(
            src_ref=window_of(lax.rem(me_b + i, n_blk)), dst_ref=wland.at[i],
            send_sem=vsend.at[0], recv_sem=vrecv.at[0], device_id=rel(i), device_id_type=MESH,
        ).start()
        return carry

    lax.fori_loop(1, n_blk, send_window, 0)
    row_wait(rarr, arecv.at[1])
    rows = dot(route_t, rarr[...].reshape(packet_rows, 128))
    lifted = jnp.concatenate([rows[0:16], rows[16:32]], axis=1).astype(BF16)
    d_pooled = jnp.concatenate([rows[32:48], rows[48:64]], axis=1).astype(BF16)

    d_means = dot_nt(d_pooled, w_down[...]) * (1.0 / 64.0)
    yrow[...] = dot(d_means.astype(BF16), perm_t[...])

    def fine_slope(g, carry):
        spreadv = expand(g).reshape(4, CH, VOX)
        for bb in range(4):
            b = 4 * g + bb
            d_mid = cot[b].astype(F32) + spreadv[bb]
            big[b] = d_mid
            value = pre[b]
            s = jax.nn.sigmoid(value)
            dpf[b] = (d_mid * (s * (1.0 + value * (1.0 - s)))).astype(BF16)
        return carry

    lax.fori_loop(0, NB // 4, fine_slope, 0)
    make_faces(dpf, faces2, pack2)
    copies4 = face_copies(land2, pack2, 1)
    for copy in copies4:
        copy.start()
    roll_taps(dpf)
    yrow[...] = dot(dot(lifted, w_up[...]).astype(BF16), perm_t[...])

    def fine_up(g, carry):
        spreadv = expand(g).reshape(4, CH, VOX)
        for bb in range(4):
            b = 4 * g + bb
            fine_out[b] = (mid[b].astype(F32) + spreadv[bb]).astype(BF16)
        return carry

    lax.fori_loop(0, NB // 4, fine_up, 0)
    rows_scale = 1.0 / math.sqrt(NB * total)
    twice = (iota((WID, VOX), 1) // 2 == iota((WID, VOX), 0)).astype(BF16)
    lifted2 = dot(lifted, twice).astype(BF16)
    up = jnp.where(iota((VOX, WID), 0) % 2 == 0, dot_tn(lifted2, d_raised[:, :WID]),
                   dot_tn(lifted2, d_raised[:, WID:])) * rows_scale
    down = dot_tn(means, d_pooled) * rows_scale
    ssrc[:, 0:16, :] = down.astype(BF16).reshape(n_blk, 16, WID)
    ssrc[:, 16:32, :] = up.astype(BF16).reshape(n_blk, 16, WID)

    def send_small(i, carry):
        pltpu.make_async_remote_copy(
            src_ref=ssrc.at[lax.rem(me_b + i, n_blk)], dst_ref=sland.at[i],
            send_sem=vsend.at[1], recv_sem=vrecv.at[1], device_id=rel(i), device_id_type=MESH,
        ).start()
        return carry

    lax.fori_loop(1, n_blk, send_small, 0)
    w_bwd = wbig[...].astype(BF16)
    gacc[...] = jnp.zeros((7 * CH, CH), F32)
    for copy in copies4:
        copy.wait_recv()
    place_faces(faces2, land2)

    def fine_backward(b, carry):
        t = full_taps(b)
        grad_fine[b] = (big[b] + dot(w_bwd, t)).astype(BF16)
        gacc[...] += dot_nt(t, fine[b])
        return carry

    lax.fori_loop(0, NB, fine_backward, 0)
    fine_bf = (gacc[...] * (1.0 / math.sqrt(NB * total * VOX))).astype(BF16)
    quarters = []
    for m in range(4):
        pick = (iota((16, CH), 1) == 4 * iota((16, CH), 0) + m).astype(BF16)
        quarters.append(dot_nt(pick, fine_bf))
    for e in range(7):
        d = 0 if e == 0 else OPPOSITE[e - 1] + 1
        fsrc[d] = jnp.concatenate(
            [quarter[:, CH * e : CH * e + CH] for quarter in quarters], axis=1).astype(BF16)
    fine_copies = [
        pltpu.make_async_remote_copy(
            src_ref=fsrc.at[t], dst_ref=fland.at[me_b], send_sem=usend.at[6 + t],
            recv_sem=vrecv.at[2], device_id=(me_s, t), device_id_type=MESH,
        )
        for t in range(7)
    ]
    for t in range(7):
        pl.when(me_b != t)(fine_copies[t].start)

    @pl.when(me_b < 7)
    def _():
        pltpu.make_async_copy(fsrc.at[lax.rem(me_b, 7)], fland.at[me_b], vrecv.at[2]).start()

    def unit_copies(kind, unit, base, slab, active):
        num = 256 * (unit - 2) - base
        low = (num + 502 + 503 * 8) // 503 - 8
        made = []
        for i in range(2):
            k = low + i
            begin = (base + 503 * k + 2560) // 256 - 10
            good = active & (k >= 0) & (k < n_blk) & (begin <= unit)
            mine = (me_s == slab) & (me_b == k)
            at = jnp.clip(unit - begin, 0, 2)
            away = pltpu.make_async_remote_copy(
                src_ref=units.at[kind], dst_ref=uland.at[at, me_s],
                send_sem=usend.at[2 * kind + i], recv_sem=urecv.at[at],
                device_id=(slab, jnp.clip(k, 0, n_blk - 1)), device_id_type=MESH,
            )
            home = pltpu.make_async_copy(units.at[kind], uland.at[at, me_s], urecv.at[at])
            pl.when(good & mine)(home.start)
            pl.when(good & jnp.logical_not(mine))(away.start)
            made.append((good & jnp.logical_not(mine), away))
        return made

    def window_wait(buf, sem):
        pltpu.make_async_copy(buf.at[pl.ds(1, n_blk - 1)], buf.at[pl.ds(1, n_blk - 1)], sem).wait()

    window_wait(sland, vrecv.at[1])
    both = lax.fori_loop(
        1, n_blk, lambda i, c: c + sland[i].astype(F32), ssrc[me_b].astype(F32)).astype(BF16)
    units[0] = both[0:16]
    units[1] = both[16:32]
    sent = unit_copies(0, me_b + 16, 2304, 0, me_b >= 0)
    sent = sent + unit_copies(1, me_b + 32, 288, n_slab - 1, me_b >= 0)

    window_wait(wland, vrecv.at[0])
    gsum[...] = lax.fori_loop(
        1, n_blk, lambda i, c: c + wland[i].astype(F32), window_of(me_b)[...].astype(F32))

    @pl.when(me_b < 7)
    def _():
        pltpu.make_async_copy(fland, fland, vrecv.at[2]).wait()
        units[2] = lax.fori_loop(
            1, n_blk, lambda i, c: c + fland[i].astype(F32), fland[0].astype(F32)).astype(BF16)

    sent = sent + unit_copies(2, me_b + 9, 2304, 0, me_b < 7)
    my_unit = (16 * skew + 503 * me_b) // 256
    for u in range(3):
        unit = my_unit + u
        small = ((me_s == 0) & (unit < 48)) | (
            (me_s == n_slab - 1) & (unit >= 32) & (unit < 64))

        @pl.when(small)
        def _():
            pltpu.make_async_copy(uland.at[u], uland.at[u], urecv.at[u]).wait()
            rows = slice(16 * u, 16 * u + 16)
            gsum[rows, :] += jnp.sum(uland[u].astype(F32), axis=0)

    down_by = skew + 503 * me_b // 16 - 16 * my_unit
    left_by = 16 * (503 * me_b % 16)
    value = pltpu.roll(gsum[...], lax.rem(48 - down_by, 48), 0)
    value = pltpu.roll(value, lax.rem(WID - left_by, WID), 1)
    below = pltpu.roll(value, 47, 0)
    grads_out[...] = jnp.where(
        iota((32, WID), 1) < WID - left_by, value[:32], below[:32])

    for copy in copies1 + copies4 + copies2 + copies3:
        copy.wait_send()
    row_wait(pk, asend.at[0])
    row_wait(rpk, asend.at[1])
    for copy in gathers:
        copy.wait_send()
    window_wait(wland, vsend.at[0])
    window_wait(sland, vsend.at[1])
    for t in range(7):
        pl.when(me_b != t)(fine_copies[t].wait_send)
    for good, copy in sent:
        pl.when(good)(copy.wait_send)


def fused(n_slab, n_blk, *operands):
    vmem = pl.BlockSpec(memory_space=pltpu.VMEM)
    smem = pl.BlockSpec(memory_space=pltpu.SMEM)
    hbm = pl.BlockSpec(memory_space=pl.ANY)
    sds = jax.ShapeDtypeStruct
    fine_like = sds((NB, CH, VOX), BF16)
    cells = sds((CELLS, WID), BF16)
    dma = pltpu.SemaphoreType.DMA
    rows = (n_blk, 16, 128)
    return pl.pallas_call(
        functools.partial(kernel, n_slab, n_blk),
        name="window",
        out_shape=(
            fine_like, cells, fine_like, cells, sds((32, WID), F32),
        ),
        in_specs=[vmem] * 7 + [hbm] + [smem] * 2 + [vmem] * 9,
        out_specs=(vmem,) * 5,
        scratch_shapes=[
            pltpu.VMEM((27 * WID, WID), BF16),
            pltpu.VMEM((SLOTS, CH, 128), BF16),
            pltpu.VMEM((SLOTS, CH, 128), BF16),
            pltpu.VMEM((2, 3, CH, 128), BF16),
            pltpu.VMEM((2, 3, CH, 128), BF16),
            pltpu.VMEM((NB, CH, 128), BF16),
            pltpu.VMEM((6, NB, CH, VOX), BF16),
            pltpu.VMEM((NB, 7 * CH, VOX), BF16),
            pltpu.VMEM((NB, CH, VOX), F32),
            pltpu.VMEM((NB, CH, VOX), BF16),
            pltpu.VMEM((NB, CH, VOX), BF16),
            pltpu.VMEM((NB, CH, VOX), F32),
            pltpu.VMEM((CELLS, VOX), F32),
            pltpu.VMEM((CELLS, VOX), F32),
            pltpu.VMEM((CH, 7 * CH), F32),
            pltpu.VMEM(rows, BF16),
            pltpu.VMEM(rows, BF16),
            pltpu.VMEM(rows, BF16),
            pltpu.VMEM(rows, BF16),
            pltpu.VMEM((8, CELLS, WID), BF16),
            pltpu.VMEM((8, CELLS, WID), BF16),
            pltpu.VMEM((CELLS, WID), BF16),
            pltpu.VMEM((CELLS, WID), BF16),
            pltpu.VMEM((7 * CH, CH), F32),
            pltpu.VMEM((6, CH, 128), BF16),
            pltpu.VMEM((6, CH, 128), BF16),
            pltpu.VMEM((CELLS, 4 * WID), BF16),
            pltpu.VMEM((n_slab, CELLS, 4 * WID), BF16),
            pltpu.VMEM((3, WID, 128), BF16),
            pltpu.VMEM((5 * WID, WID), BF16),
            pltpu.VMEM((n_blk, 48, WID), BF16),
            pltpu.VMEM((n_blk, 32, WID), BF16),
            pltpu.VMEM((n_blk, 32, WID), BF16),
            pltpu.VMEM((7, 16, WID), BF16),
            pltpu.VMEM((n_blk, 16, WID), BF16),
            pltpu.VMEM((3, 16, WID), BF16),
            pltpu.VMEM((3, n_slab, 16, WID), BF16),
            pltpu.VMEM((48, WID), F32),
            dma, dma((4,)), dma((4,)), dma((2,)), dma((2,)), dma((16,)), dma((16,)),
            dma((n_slab - 1,)), dma, dma((2,)), dma((3,)), dma((13,)), dma((3,)),
        ],
        compiler_params=pltpu.CompilerParams(
            collective_id=0, has_side_effects=True, vmem_limit_bytes=56 * 1024 * 1024
        ),
    )(*operands)


def face_routes(neighbors, position):
    opposite = jnp.array(OPPOSITE, jnp.int32)
    present = neighbors >= 0
    relation = jnp.where(present, neighbors // NB - position, 5).reshape(-1)
    lookup = (jnp.where(present, neighbors % NB, 0) * 6 + opposite[None, :]).reshape(-1)
    ids = jnp.arange(FACES, dtype=jnp.int32)
    send = []
    code = jnp.where(relation == 0, 2 * lookup, 2 * ZERO)
    for step, base in ((-1, PREV0), (1, NEXT0)):
        chosen = relation == step
        place = jnp.sum((chosen[None, :] & (ids[None, :] < ids[:, None])).astype(jnp.int32), axis=1)
        hit = chosen[None, :] & (place[None, :] == jnp.arange(FB, dtype=jnp.int32)[:, None])
        send.append(ZERO + jnp.sum(jnp.where(hit, ids[None, :] - ZERO, 0), axis=1))
        rank = jnp.sum(
            ((lookup[None, :] < lookup[:, None]) & chosen[None, :]).astype(jnp.int32), axis=1)
        code = jnp.where(chosen, 2 * base + rank, code)
    return jnp.concatenate(send), code


def shards(
    n_slab, n_blk,
    fine_in, latent, w_fine, w_down, w_coarse, w_up, neighbors, pool_owner, pool_cell, cot_fine,
    cot_coarse,
):
    position = lax.axis_index(("slab", "blk"))
    send, code = face_routes(neighbors, position)
    pad = lambda a: jnp.pad(a.reshape(NB, 1), ((0, CELLS - NB), (0, 0)))
    outs = fused(
        n_slab, n_blk,
        fine_in, cot_fine, latent.reshape(CELLS, WID), cot_coarse.reshape(CELLS, WID),
        w_fine, w_down, w_up, w_coarse, send, code, pad(pool_owner), pad(pool_cell), *tables())
    fine_out, c_out, grad_fine, g_lat, grads = outs
    weight_grads = grads.reshape(-1)[:SHARD]
    return (fine_out, c_out.reshape(latent.shape), grad_fine, g_lat.reshape(latent.shape),
            weight_grads)


def solution(mesh):
    n_slab, n_blk = mesh.shape["slab"], mesh.shape["blk"]
    return jax.shard_map(
        functools.partial(shards, n_slab, n_blk),
        mesh=mesh,
        in_specs=(
            P(("slab", "blk"), None, None), P("slab", "blk", None, None), P(), P(), P(), P(),
            P(("slab", "blk"), None), P(("slab", "blk"), None), P(("slab", "blk")),
            P(("slab", "blk"), None, None), P("slab", "blk", None, None),
        ),
        out_specs=(
            P(("slab", "blk"), None, None), P("slab", "blk", None, None),
            P(("slab", "blk"), None, None), P("slab", "blk", None, None), P(("slab", "blk")),
        ),
        check_vma=False,
    )
```

time: 551 us -> 108 us (0.20); the launches traced: 542 us -> 107 us
  waiting for transfers between devices: 240 us -> 0 us
  matrix products: 91.3 us -> 0 us
  Pallas kernels: 0 us -> 90.2 us
  starting transfers between devices: 85.2 us -> 0 us
  local copies, waits for them, and re-layouts: 85.4 us -> 13.2 us
  other arithmetic: 23.3 us -> 2.97 us
  between operations: 15.9 us -> 0.69 us
    unnamed x2 -> x0, waiting for transfers between devices: 237 us -> none
    dot_general x76 -> x0, matrix products: 91.3 us -> none  [the longest x6 21.6 us: fine_transpose(): jnp.einsum('bov,ko->bkv', back_list[OPPOSITE[direction]], block_w, prefer...]
    pallas_call x0 -> x1, Pallas kernels: none -> 90.2 us  [fused(): pl.pallas_call(functools.partial(kernel, n_slab, n_blk), name='window', o...]
    all_to_all x5 -> x0, starting transfers between devices: 50.8 us -> none  [the longest x4 39.5 us: swap_rows(): lax.all_to_all(packed, 'blk', split_axis=0, concat_axis=0, tiled=True)]
    ppermute x12 -> x0, starting transfers between devices: 34.2 us -> none  [the longest x6 21.8 us: extended_2(): lax.ppermute(tail, axis, [(i, (i + 1) % count) for i in range(ends)])]
    reshape x15 -> x1, local copies, waits for them, and re-layouts: 21.7 us -> 0.74 us  [shards(): pad = lambda a: jnp.pad(a.reshape(NB, 1), ((0, CELLS - NB), (0, 0)))]
    transpose x9 -> x0, local copies, waits for them, and re-layouts: 17.3 us -> none  [coarse_transpose(): block_w = weight[offset:offset + 3 * width_c].reshape(3, width_c, width_c...]
    slice x15 -> x0, local copies, waits for them, and re-layouts: 14 us -> none  [the longest x3 4.31 us: shifted(): moved = jnp.concatenate([tensor[:, :, stride:], filler], axis=2)]
  transfers between devices with their start and end apart: 18 -> 0, of which waited for: 3 -> 0; matrix products, arithmetic and copies ran while one was open for 28% -> 0% of each run, Pallas kernels for 0% -> 0%
where the time goes in v1:
time: 108 us; the launch traced here: 107 us
  Pallas kernels  90.2 us (84%)
  local copies, waits for them, and re-layouts  13.2 us (12%)
  other arithmetic  2.97 us (3%)
    pallas_call x1, Pallas kernels, fused(): pl.pallas_call(functools.partial(kernel, n_slab, n_blk), name='window', o...  90.2 us
    unnamed x7, local copies, waits for them, and re-layouts  10.4 us

profile of v1, /device:TPU:32, one launch (start us, length us, event | category | flops | bytes accessed | tf_op | source)
XLA Modules:
  0.0 107.1 jit_solution(16368506153386695054)
XLA Ops:
  0.6 0.8 fusion.6
  1.4 0.1 copy.40
  1.5 0.1 lt.30
  1.6 0.7 broadcast_compare_fusion.2
  2.3 0.1 copy.41
  2.4 0.1 eq.68
  2.5 0.1 copy.38
  2.6 0.1 eq.58
  2.7 0.1 copy.39
  2.8 0.1 eq.63
  2.9 0.2 convert_reduce_fusion.1
  3.2 0.5 select_select_fusion.code_sm
  3.7 0.1 select_reduce_fusion.1
  3.8 0.6 pad_add_fusion.send_sm
  4.4 0.7 copy.42
  5.2 0.6 pad.7.owner
  5.8 0.7 copy.43
  6.5 0.6 pad.8.cell
  7.1 1.6 %copy.44.w_fine = bf16[448,64]{1,0:T(8,128)(2,1)} copy(bf16[448,64]{0,1:T(8,128)(2,1)} %param.21) | data formatting | bytes 114688 | tf_op args[2]
  8.7 90.2 %window.1 = (bf16[12,64,512]{2,1,0:T(8,128)(2,1)}, bf16[16,256]{1,0:T(8,128)(2,1)}, bf16[12,64,512]{2,1,0:T(8,128)(2,1)}, bf16[16,256]{1,0:T(8,128)(2,1)}, f32[32,256]{1,0:T(8,128)}) custom-call(bf16[12,64,512]{2,1,0:T(8,128)(2,1)} %fine.1, bf16[12,64,512]{2,1,0:T(8,128)(2,1)} %cot.1, bf16[16,256]{1,0:T(8,128)(2,1)} %bitcast.12, bf16[16,256]{1,0:T(8,128)(2,1)} %bitcast.13, ...), custom_call_target="tpu_custom_call" | custom-call | tf_op jit(solution)/shard_map/window/pallas_call | solution.py:581
  99.0 1.4 %copy.45 = f32[4,2,8,128]{3,1,2,0:T(2,128)} copy(f32[4,2,8,128]{3,2,1,0:T(8,128)} %bitcast.9) | data formatting | bytes 65536
  100.4 2.1 %copy.50 = bf16[12,64,512]{2,1,0:T(8,128)(2,1)} copy(bf16[12,64,512]{2,1,0:T(8,128)(2,1)} %get-tuple-element.32) | data formatting | bytes 1572864
  102.4 1.3 %copy.51 = bf16[1,1,16,256]{3,2,1,0:T(8,128)(2,1)} copy(bf16[1,1,16,256]{3,2,1,0:T(8,128)(2,1)} %bitcast.11) | data formatting | bytes 16384
  103.7 2.1 %copy.52 = bf16[12,64,512]{2,1,0:T(8,128)(2,1)} copy(bf16[12,64,512]{2,1,0:T(8,128)(2,1)} %get-tuple-element.34) | data formatting | bytes 1572864
  105.8 1.3 %copy.53 = bf16[1,1,16,256]{3,2,1,0:T(8,128)(2,1)} copy(bf16[1,1,16,256]{3,2,1,0:T(8,128)(2,1)} %bitcast.10) | data formatting | bytes 16384
  (3 shorter events, 0.0 us)

commit v2 on v1

v2 whole, which is shorter than its diff:
```python
import functools
import math

import jax
import jax.numpy as jnp
import numpy as np
from jax import lax
from jax.experimental import pallas as pl
from jax.experimental.pallas import tpu as pltpu
from jax.sharding import PartitionSpec as P

NB = 12
CH = 64
VOX = 512
WID = 256
CELLS = 16
FB = 6
OPPOSITE = (1, 0, 3, 2, 5, 4)
STRIDES = (64, 8, 1)
FACES = NB * 6
PREV0 = FACES
NEXT0 = FACES + 3
ZERO = FACES + 6
SLOTS = FACES + 7
OFFSETS = ((-1, -1), (-1, 0), (-1, 1), (0, -1), (0, 1), (1, -1), (1, 0), (1, 1))
SHARD = 8048
SLAB_ROWS = 1006
MESH = pl.DeviceIdType.MESH
F32 = jnp.float32
BF16 = jnp.bfloat16


def tables():
    voxel = np.arange(VOX)
    coords = (voxel // 64, voxel // 8 % 8, voxel % 8)
    octant = 4 * (coords[0] // 4) + 2 * (coords[1] // 4) + coords[2] // 4
    pull = np.zeros((VOX, 6 * 128), np.float32)
    place = np.zeros((6, 128, VOX), np.float32)
    keep = np.ones((6, 1, VOX), np.float32)
    for axis in range(3):
        others = [coords[other] for other in range(3) if other != axis]
        index = others[0] * 8 + others[1]
        for side in range(2):
            d = 2 * axis + side
            on = coords[axis] == 7 * side
            keep[d, 0, on] = 0.0
            for half in range(2):
                pull[voxel[on], 128 * d + 64 * half + index[on]] = 1.0
                place[d, 64 * half + index[on], voxel[on]] = 1.0
    spread = (octant[:, None] == np.arange(VOX)[None, :] // 64).astype(np.float32)
    major = np.arange(VOX)
    perm = np.zeros((VOX, VOX), np.float32)
    perm[major, 8 * (major % 64) + major // 64] = 1.0
    bf = lambda a: jnp.asarray(a, BF16)
    return bf(pull), bf(place.reshape(6 * 128, VOX)), jnp.asarray(keep), bf(spread), bf(spread.T), bf(perm), bf(perm.T)


def dot(a, b):
    return jnp.dot(a, b, preferred_element_type=F32)


def dot_nt(a, b):
    return lax.dot_general(a, b, (((1,), (1,)), ((), ())), preferred_element_type=F32)


def dot_tn(a, b):
    return lax.dot_general(a, b, (((0,), (0,)), ((), ())), preferred_element_type=F32)


def iota(shape, dim):
    return lax.broadcasted_iota(jnp.int32, shape, dim)


def kernel(
    n_slab, n_blk,
    fine_hbm, cot_hbm, latent, cotc, w_fwd, w_down_hbm, w_up_hbm, w_coarse_hbm, nbr, owner, cell,
    pull_hbm, place_hbm, keep, spread_hbm, spread_t_hbm, perm_hbm, perm_t_hbm,
    fine_out_hbm, coarse_out, grad_fine_hbm, grad_latent, grads_out,
    fine, cot, w_down, w_up, w_coarse, pull, place, spread, spread_t, perm, perm_t,
    fine_out, grad_fine, faces1, faces2, faces_wide, pack1, pack2, land1, land2, half, near, zall,
    taps, pre, mid, dpf, big, ysum, yrow, w_bwd, route_pk, arr_a, arr_b, pk_a, pk_b, rpk, rarr,
    rim1, rim2, rimsrc1, rimsrc2, gacc, xsrc, dsrc, upsrc, downsrc, xgat, dgat, upgat, downgat,
    dco, xq, gbuf, wland, fsrc, fland, unit_ref, uland, gsum, idx_v, idx_s,
    wsem, isem, osem, fsend, frecv, asend, arecv, rsend, rrecv, csend, crecv, vsend, vrecv,
    usend, urecv,
):
    me_s = lax.axis_index("slab")
    me_b = lax.axis_index("blk")
    total = n_slab * n_blk
    pos = me_s * n_blk + me_b
    after = lax.rem(pos + 1, total)
    before = lax.rem(pos + total - 1, total)
    rel = lambda i: (me_s, lax.rem(me_b + i, n_blk))
    column = lambda i: (lax.rem(me_s + i, n_slab), me_b)
    flat = lambda k: (lax.div(k, n_blk), lax.rem(k, n_blk))
    near_id = lambda a, b: (lax.rem(me_s + a + n_slab, n_slab), lax.rem(me_b + b + n_blk, n_blk))

    loads = {}
    for i, (name, src, dst) in enumerate((
        ("fine", fine_hbm, fine), ("pull", pull_hbm, pull), ("cot", cot_hbm, cot),
        ("spread", spread_hbm, spread), ("perm", perm_hbm, perm), ("place", place_hbm, place),
        ("up", w_up_hbm, w_up), ("down", w_down_hbm, w_down), ("coarse", w_coarse_hbm, w_coarse),
        ("perm_t", perm_t_hbm, perm_t), ("spread_t", spread_t_hbm, spread_t),
    )):
        loads[name] = pltpu.make_async_copy(src, dst, wsem.at[i])
        loads[name].start()

    barrier = pltpu.get_barrier_semaphore()

    def greet(i, carry):
        pl.semaphore_signal(barrier, inc=1, device_id=rel(i), device_id_type=MESH)
        return carry

    lax.fori_loop(1, n_blk, greet, 0)
    for i in range(1, n_slab):
        pl.semaphore_signal(barrier, inc=1, device_id=column(i), device_id_type=MESH)
    for a, b in OFFSETS:
        if a != 0 and b != 0:
            pl.semaphore_signal(barrier, inc=1, device_id=near_id(a, b), device_id_type=MESH)
    for k in (before, after):
        pl.semaphore_signal(barrier, inc=1, device_id=flat(k), device_id_type=MESH)

    lane1 = iota((1, 128), 1)
    lane = iota((128, 128), 1)
    sub = iota((128, 128), 0)
    diagonal = lane == sub
    ints = lambda m: m.astype(jnp.int32)
    as_col = lambda row: jnp.sum(jnp.where(diagonal, row, 0), axis=1, keepdims=True)
    down_sum = lambda m: jnp.sum(ints(m), axis=0, keepdims=True)
    number = jnp.full((1, 128), -1, jnp.int32)
    key = jnp.full((1, 128), 0, jnp.int32)
    for d in range(6):
        for b in range(NB):
            value = nbr[d, b]
            here = lane1 == d * NB + b
            number = jnp.where(here, value, number)
            key = jnp.where(here, value + NB * OPPOSITE[d], key)
    low = NB * pos
    code = jnp.full((1, 128), 2 * ZERO, jnp.int32)
    code = jnp.where((number >= low) & (number < low + NB), 2 * (key - low), code)
    for i, base in ((-1, PREV0), (1, NEXT0)):
        first = low + i * NB
        chosen = (number >= first) & (number < first + NB) & (number >= 0)
        ranked = jnp.where(chosen, key - first, 10000)
        rank = down_sum(as_col(ranked) < ranked)
        code = jnp.where(chosen, 2 * base + rank, code)
        mine = down_sum((as_col(ints(chosen)) == 1) & (sub < lane))
        order = as_col(jnp.where(chosen, mine, -1))
        sends = jnp.sum(jnp.where(order == lane, sub - ZERO, 0), axis=0, keepdims=True) + ZERO
        row = 1 if i == -1 else 2
        idx_v[row : row + 1, :] = jnp.clip(sends, 0, ZERO)
    idx_v[0:1, :] = jnp.clip(code, 0, 2 * ZERO)
    load_idx = pltpu.make_async_copy(idx_v, idx_s, isem)
    load_idx.start()

    lane64 = iota((CH, 128), 1) // 64
    half[0] = (lane64 == 0).astype(BF16)
    half[1] = (lane64 == 1).astype(BF16)
    eye = (iota((CH, VOX), 1) % 64 == iota((CH, VOX), 0)).astype(F32)

    def make_faces(src, faces, wide):
        faces[ZERO] = jnp.zeros((CH, 128), BF16)
        for g in range(NB // 4):
            rows = src[4 * g : 4 * g + 4].reshape(4 * CH, VOX)
            out = dot(rows, pull[...]).astype(BF16)
            for bb in range(4):
                b = 4 * g + bb
                for d in range(6):
                    part = out[CH * bb : CH * bb + CH, 128 * d : 128 * d + 128]
                    faces[d * NB + b] = part
                    if wide is not None:
                        wide[d, :, 128 * b : 128 * b + 128] = part

    def make_packs(faces, pack):
        for s in range(2):
            for q in range(3):
                first = faces[idx_s[1 + s, 2 * q]]
                second = faces[idx_s[1 + s, 2 * q + 1]]
                pack[s, q] = first * half[0] + second * half[1]

    def face_copies(land, pack, k):
        return [
            pltpu.make_async_remote_copy(
                src_ref=pack.at[0], dst_ref=land.at[pl.ds(3, 3)],
                send_sem=fsend.at[2 * k], recv_sem=frecv.at[2 * k],
                device_id=flat(before), device_id_type=MESH,
            ),
            pltpu.make_async_remote_copy(
                src_ref=pack.at[1], dst_ref=land.at[pl.ds(0, 3)],
                send_sem=fsend.at[2 * k + 1], recv_sem=frecv.at[2 * k + 1],
                device_id=flat(after), device_id_type=MESH,
            ),
        ]

    def roll_taps(src, b):
        x = src[b]
        wide = x.astype(F32)
        taps[b, 0:CH, :] = x
        for d in range(6):
            stride = STRIDES[d // 2]
            moved = pltpu.roll(wide, stride if d % 2 == 0 else VOX - stride, 1)
            taps[b, CH * (d + 1) : CH * (d + 2), :] = (moved * keep[d]).astype(BF16)

    def gather_faces(faces, land):
        faces[PREV0 : PREV0 + 6] = land[...]
        for d in range(6):
            for b in range(NB):
                at = idx_s[0, d * NB + b]
                near[d, :, 128 * b : 128 * b + 128] = (
                    faces[lax.shift_right_logical(at, 1)] * half[lax.bitwise_and(at, 1)])

    def weigh_faces(w):
        for d in range(6):
            z = dot(w[:, CH * (d + 1) : CH * (d + 2)], near[d]).astype(BF16)
            for b in range(NB):
                zall[b, :, 128 * d : 128 * d + 128] = z[:, 128 * b : 128 * b + 128]

    def placed(g):
        return dot(zall[pl.ds(4 * g, 4)].reshape(4 * CH, 6 * 128), place[...])

    def octant_rows(src):
        for g in range(NB // 4):
            rows = src[4 * g : 4 * g + 4].reshape(4 * CH, VOX)
            sums = dot(rows, spread[...])
            for bb in range(4):
                part = sums[CH * bb : CH * bb + CH] * eye
                ysum[4 * g + bb : 4 * g + bb + 1, :] = jnp.sum(part, axis=0, keepdims=True)
        return ysum[...]

    def expand(g):
        parts = []
        for bb in range(4):
            row = yrow[pl.ds(4 * g + bb, 1), :]
            parts.append((row * eye).astype(BF16))
        return dot(jnp.concatenate(parts, axis=0), spread_t[...])

    def row_wait(buf, sem):
        pltpu.make_async_copy(buf.at[pl.ds(1, n_blk - 1)], buf.at[pl.ds(1, n_blk - 1)], sem).wait()

    def send_rows(src, dst, back, k):
        def body(i, carry):
            pltpu.make_async_remote_copy(
                src_ref=src.at[i], dst_ref=dst.at[i], send_sem=asend.at[k], recv_sem=arecv.at[k],
                device_id=rel(n_blk - i if back else i), device_id_type=MESH,
            ).start()
            return carry

        lax.fori_loop(1, n_blk, body, 0)

    loads["fine"].wait()
    loads["pull"].wait()
    make_faces(fine, faces1, faces_wide)
    load_idx.wait()
    make_packs(faces1, pack1)
    pl.semaphore_wait(barrier, n_blk - 1 + n_slab - 1 + 4 + 2)
    copies1 = face_copies(land1, pack1, 0)
    for copy in copies1:
        copy.start()

    packet_rows = n_blk * 16
    sub16 = iota((CELLS, 128), 0)
    lane16 = iota((CELLS, 128), 1)
    own_col = jnp.full((CELLS, 128), 0, jnp.int32)
    cell_col = jnp.full((CELLS, 128), -1, jnp.int32)
    for b in range(NB):
        own_col = jnp.where(sub16 == b, owner[b], own_col)
        cell_col = jnp.where(sub16 == b, cell[b], cell_col)
    own_row = jnp.sum(jnp.where(sub16 == lane16, own_col, 0), axis=0, keepdims=True)
    same = (own_col == own_row) & (lane16 < sub16)
    slot = jnp.sum(same.astype(jnp.int32), axis=1, keepdims=True)
    gap = own_col[:, :1] - me_b
    ahead = jnp.where(gap < 0, gap + n_blk, gap)
    start = jnp.where(iota((CELLS, 1), 0) < NB, ahead * 16 + 5 * slot, -1000)
    start_col = jnp.concatenate([start + j for j in range(5)] + [start * 0 - 1000] * 3, axis=0)
    route_t = (iota((128, packet_rows), 1) == start_col).astype(BF16)
    start_row = jnp.sum(jnp.where(diagonal, start_col, 0), axis=0, keepdims=True)
    route_pk[...] = (iota((packet_rows, 128), 0) == start_row).astype(BF16)
    cell_hot = (lane16 == cell_col).astype(F32)

    def packets(rows, last):
        wide = rows.astype(F32)
        payload = jnp.concatenate(
            [wide[:, 128 * j : 128 * j + 128] for j in range(4)]
            + [last, jnp.zeros((48, 128), F32)], axis=0).astype(BF16)
        return dot(route_pk[...], payload).astype(BF16).reshape(n_blk, 16, 128)

    ysum[...] = jnp.zeros((CELLS, VOX), F32)
    loads["cot"].wait()
    loads["spread"].wait()
    loads["perm"].wait()
    d_raised = dot(octant_rows(cot).astype(BF16), perm[...]).astype(BF16)
    pk_a[...] = packets(d_raised, cell_hot)
    arr_a[0] = pk_a[0]
    send_rows(pk_a, arr_a, False, 0)

    for e in range(7):
        d = 0 if e == 0 else OPPOSITE[e - 1] + 1
        w_bwd[:, CH * e : CH * e + CH] = w_fwd[:, CH * d : CH * d + CH].astype(F32).T

    def own_forward(b, carry):
        roll_taps(fine, b)
        pre[b] = dot(w_fwd[...], taps[b])
        return carry

    lax.fori_loop(0, NB, own_forward, 0)
    loads["place"].wait()
    for copy in copies1:
        copy.wait_recv()
    gather_faces(faces1, land1)
    weigh_faces(w_fwd[...])

    def fine_forward(g, carry):
        more = placed(g).reshape(4, CH, VOX)
        for bb in range(4):
            b = 4 * g + bb
            value = pre[b] + more[bb]
            pre[b] = value
            mid[b] = (fine[b].astype(F32) + value * jax.nn.sigmoid(value)).astype(BF16)
        return carry

    lax.fori_loop(0, NB // 4, fine_forward, 0)
    means = dot((octant_rows(mid) * (1.0 / 64.0)).astype(BF16), perm[...]).astype(BF16)
    pk_b[...] = packets(means, jnp.zeros((CELLS, 128), F32))
    arr_b[0] = pk_b[0]
    send_rows(pk_b, arr_b, False, 1)

    def lined(arr):
        wide = arr[...].reshape(packet_rows, 128).astype(F32)
        return jnp.concatenate([pltpu.roll(wide, 4 - j, 0) for j in range(4)], axis=1).astype(BF16)

    def two_parts(x):
        high = x.astype(BF16)
        return high, (x - high.astype(F32)).astype(BF16)

    row_wait(arr_a, arecv.at[0])
    row_of = iota((packet_rows, 128), 0) % 16
    hot = jnp.where(
        (row_of == 4) | (row_of == 9), arr_a[...].reshape(packet_rows, 128).astype(F32), 0.0)
    hot_t = hot.T[:CELLS].astype(BF16)
    hot16 = hot.astype(BF16)
    raised_hi, raised_lo = two_parts(dot(hot_t, lined(arr_a)))
    loads["up"].wait()
    lift = dot_nt(jnp.concatenate([raised_hi, raised_lo], axis=0), w_up[...])
    dco[...] = cotc[...].astype(F32) + lift[:CELLS] + lift[CELLS:]
    loads["down"].wait()

    row_wait(arr_b, arecv.at[1])
    means_hi, means_lo = two_parts(dot(hot_t, lined(arr_b)))
    pooled = dot(jnp.concatenate([means_hi, means_lo], axis=0), w_down[...])
    c_in = (latent[...].astype(F32) + pooled[:CELLS] + pooled[CELLS:]).astype(BF16)

    def rim_copies(src, dst, k):
        return [
            pltpu.make_async_remote_copy(
                src_ref=src, dst_ref=dst.at[7 - i], send_sem=rsend.at[8 * k + i],
                recv_sem=rrecv.at[8 * k + 7 - i], device_id=near_id(a, b), device_id_type=MESH,
            )
            for i, (a, b) in enumerate(OFFSETS)
        ]

    def rim_tile(dst, own, a, b):
        if a == 0 and b == 0:
            return own.astype(F32)
        zz, yy = me_s + a, me_b + b
        inside = (zz >= 0) & (zz < n_slab) & (yy >= 0) & (yy < n_blk)
        tile = dst[OFFSETS.index((a, b))].astype(F32)
        return tile * jnp.where(inside, 1.0, 0.0)

    sub_x = iota((CELLS, WID), 0)

    def along_x(tile, step):
        if step == 0:
            return tile
        moved = pltpu.roll(tile, 1 if step == -1 else CELLS - 1, 0)
        return jnp.where(sub_x == (0 if step == -1 else CELLS - 1), 0.0, moved)

    def column_copies(src, dst, k):
        made = [
            pltpu.make_async_remote_copy(
                src_ref=src, dst_ref=dst.at[me_s], send_sem=csend.at[8 * k + i],
                recv_sem=crecv.at[k], device_id=column(i), device_id_type=MESH,
            )
            for i in range(1, n_slab)
        ]
        pltpu.make_async_copy(src, dst.at[me_s], crecv.at[k]).start()
        for copy in made:
            copy.start()
        return made

    def plane_copy(src, dst, slab, k):
        copy = pltpu.make_async_remote_copy(
            src_ref=src, dst_ref=dst.at[me_s], send_sem=csend.at[8 * k], recv_sem=crecv.at[k],
            device_id=(slab, me_b), device_id_type=MESH,
        )
        pl.when(me_s != slab)(copy.start)
        pl.when(me_s == slab)(pltpu.make_async_copy(src, dst.at[me_s], crecv.at[k]).start)
        return copy

    rimsrc1[...] = c_in
    copies2 = rim_copies(rimsrc1, rim1, 0)
    for copy in copies2:
        copy.start()
    loads["coarse"].wait()
    for copy in copies2:
        copy.wait_recv()
    xsrc[...] = jnp.concatenate(
        [rim_tile(rim1, c_in, 0, q - 1) for q in range(3)], axis=1).astype(BF16)
    x_sent = column_copies(xsrc, xgat, 0)
    acc = jnp.zeros((CELLS, WID), F32)
    for p in range(3):
        for q in range(3):
            tile = rim_tile(rim1, c_in, p - 1, q - 1)
            row = jnp.concatenate([along_x(tile, r - 1) for r in range(3)], axis=1).astype(BF16)
            base = (p * 3 + q) * 3 * WID
            acc = acc + dot(row, w_coarse[base : base + 3 * WID, :])
    sig = jax.nn.sigmoid(acc)
    d_pre = (dco[...] * (sig * (1.0 + acc * (1.0 - sig)))).astype(BF16)
    rimsrc2[...] = d_pre
    copies3 = rim_copies(rimsrc2, rim2, 1)
    for copy in copies3:
        copy.start()
    c_out = (c_in.astype(F32) + acc * sig).astype(BF16)
    coarse_out[...] = c_out
    dsrc[...] = d_pre
    d_sent = column_copies(dsrc, dgat, 1)
    upsrc[...] = jnp.concatenate([c_out.astype(F32), raised_hi.astype(F32)], axis=1).astype(BF16)
    up_sent = plane_copy(upsrc, upgat, n_slab - 1, 2)
    for copy in copies3:
        copy.wait_recv()
    acc = jnp.zeros((CELLS, WID), F32)
    for p in range(3):
        for q in range(3):
            tile = rim_tile(rim2, d_pre, 1 - p, 1 - q)
            for r in range(3):
                base = ((p * 3 + q) * 3 + r) * WID
                moved = along_x(tile, 1 - r).astype(BF16)
                acc = acc + dot_nt(moved, w_coarse[base : base + WID, :])
    g_lat = (dco[...] + acc).astype(BF16)
    grad_latent[...] = g_lat

    grid = jnp.concatenate([c_out.astype(F32), g_lat.astype(F32)], axis=1)
    grid = jnp.concatenate([grid, jnp.zeros((128 - CELLS, 2 * WID), F32)], axis=0).astype(BF16)
    picked = dot(hot16, grid)
    back = jnp.zeros((packet_rows, 128), F32)
    for j in range(4):
        back = back + pltpu.roll(picked[:, 128 * j : 128 * j + 128], packet_rows - 4 + j, 0)
    rpk[...] = back.astype(BF16).reshape(n_blk, 16, 128)
    rarr[0] = rpk[0]
    send_rows(rpk, rarr, True, 2)
    downsrc[...] = jnp.concatenate([g_lat.astype(F32), means_hi.astype(F32)], axis=1).astype(BF16)
    down_sent = plane_copy(downsrc, downgat, 0, 3)

    base_row = me_s * SLAB_ROWS + 144
    first_tap = base_row // WID - 3
    skew = base_row % WID
    pltpu.make_async_copy(xgat, xgat, crecv.at[0]).wait()
    everything = xgat[...].reshape(n_slab * CELLS, 3 * WID).astype(F32)
    for q in range(3):
        xq[q] = everything[:, q * WID : q * WID + WID].T.astype(BF16)
    pltpu.make_async_copy(dgat, dgat, crecv.at[1]).wait()
    d_all = dgat[...].reshape(n_slab * CELLS, WID)

    def tap_rows(i, carry):
        t = first_tap + i
        inside = (t >= 0) & (t < 27)
        tc = jnp.clip(t, 0, 26)
        p, q, r = tc // 9, tc // 3 % 3, tc % 3
        shift = (sub // 16 == lane // 16 + p - 1) & (sub % 16 == lane % 16 + r - 1)
        moved = dot(xq[q], shift.astype(BF16)).astype(BF16)
        gbuf[pl.ds(pl.multiple_of(i * WID, WID), WID), :] = (
            dot(moved, d_all) * jnp.where(inside, 1.0 / math.sqrt(CELLS * total), 0.0)
        ).astype(BF16)
        return carry

    lax.fori_loop(0, 5, tap_rows, 0)
    rows_scale = 1.0 / math.sqrt(NB * total)

    @pl.when(me_s == n_slab - 1)
    def _():
        pltpu.make_async_copy(upgat, upgat, crecv.at[2]).wait()
        left = upgat[:, :, :WID].reshape(n_slab * CELLS, WID)
        twice = (iota((WID, VOX), 1) // 2 == iota((WID, VOX), 0)).astype(BF16)
        left = dot(left, twice).astype(BF16)
        right = upgat[:, :, WID:].reshape(n_slab * CELLS, VOX)
        up = jnp.where(iota((VOX, WID), 0) % 2 == 0, dot_tn(left, right[:, :WID]),
                       dot_tn(left, right[:, WID:]))
        gbuf[512:1024, :] = (up * rows_scale).astype(BF16)

    @pl.when(me_s == 0)
    def _():
        pltpu.make_async_copy(downgat, downgat, crecv.at[3]).wait()
        left = downgat[:, :, WID:].reshape(n_slab * CELLS, VOX)
        right = downgat[:, :, :WID].reshape(n_slab * CELLS, WID)
        gbuf[256:768, :] = (dot_tn(left, right) * rows_scale).astype(BF16)

    def window_of(k):
        unit = (16 * skew + 503 * k) // 256
        return gbuf.at[pl.ds(pl.multiple_of(16 * unit, 16), 48)]

    def send_window(i, carry):
        pltpu.make_async_remote_copy(
            src_ref=window_of(lax.rem(me_b + i, n_blk)), dst_ref=wland.at[i],
            send_sem=vsend, recv_sem=vrecv.at[0], device_id=rel(i), device_id_type=MESH,
        ).start()
        return carry

    lax.fori_loop(1, n_blk, send_window, 0)
    loads["perm_t"].wait()
    loads["spread_t"].wait()
    row_wait(rarr, arecv.at[2])
    rows = dot(route_t, rarr[...].reshape(packet_rows, 128))
    lifted = jnp.concatenate([rows[0:16], rows[16:32]], axis=1).astype(BF16)
    d_pooled = jnp.concatenate([rows[32:48], rows[48:64]], axis=1).astype(BF16)

    d_means = dot_nt(d_pooled, w_down[...]) * (1.0 / 64.0)
    yrow[...] = dot(d_means.astype(BF16), perm_t[...])

    def fine_slope(g, carry):
        spreadv = expand(g).reshape(4, CH, VOX)
        for bb in range(4):
            b = 4 * g + bb
            d_mid = cot[b].astype(F32) + spreadv[bb]
            big[b] = d_mid
            value = pre[b]
            s = jax.nn.sigmoid(value)
            dpf[b] = (d_mid * (s * (1.0 + value * (1.0 - s)))).astype(BF16)
        return carry

    lax.fori_loop(0, NB // 4, fine_slope, 0)
    make_faces(dpf, faces2, None)
    make_packs(faces2, pack2)
    copies4 = face_copies(land2, pack2, 1)
    for copy in copies4:
        copy.start()
    w_back = w_bwd[...].astype(BF16)
    gacc[...] = jnp.zeros((7 * CH, CH), F32)

    def own_backward(b, carry):
        roll_taps(dpf, b)
        t = taps[b]
        big[b] += dot(w_back, t)
        gacc[...] += dot_nt(t, fine[b])
        return carry

    lax.fori_loop(0, NB, own_backward, 0)
    for copy in copies4:
        copy.wait_recv()
    gather_faces(faces2, land2)
    for e in range(6):
        gacc[CH * (e + 1) : CH * (e + 2), :] += dot_nt(near[e], faces_wide[e])
    fine_bf = (gacc[...] * (1.0 / math.sqrt(NB * total * VOX))).astype(BF16)
    quarters = []
    for m in range(4):
        pick = (iota((16, CH), 1) == 4 * iota((16, CH), 0) + m).astype(BF16)
        quarters.append(dot_nt(pick, fine_bf))
    for e in range(7):
        d = 0 if e == 0 else OPPOSITE[e - 1] + 1
        fsrc[d] = jnp.concatenate(
            [quarter[:, CH * e : CH * e + CH] for quarter in quarters], axis=1).astype(BF16)
    fine_copies = [
        pltpu.make_async_remote_copy(
            src_ref=fsrc.at[t], dst_ref=fland.at[me_b], send_sem=usend.at[2 + t],
            recv_sem=vrecv.at[1], device_id=(me_s, t), device_id_type=MESH,
        )
        for t in range(7)
    ]
    for t in range(7):
        pl.when(me_b != t)(fine_copies[t].start)

    @pl.when(me_b < 7)
    def _():
        pltpu.make_async_copy(fsrc.at[lax.rem(me_b, 7)], fland.at[me_b], vrecv.at[1]).start()

    weigh_faces(w_back)

    def fine_backward(g, carry):
        more = placed(g).reshape(4, CH, VOX)
        for bb in range(4):
            b = 4 * g + bb
            grad_fine[b] = (big[b] + more[bb]).astype(BF16)
        return carry

    lax.fori_loop(0, NB // 4, fine_backward, 0)
    store_grad = pltpu.make_async_copy(grad_fine, grad_fine_hbm, osem.at[0])
    store_grad.start()

    @pl.when(me_b < 7)
    def _():
        pltpu.make_async_copy(fland, fland, vrecv.at[1]).wait()
        unit_ref[...] = lax.fori_loop(
            1, n_blk, lambda i, c: c + fland[i].astype(F32), fland[0].astype(F32)).astype(BF16)

    unit = me_b + 9
    low = (256 * (unit - 2) - 2304 + 502 + 503 * 8) // 503 - 8
    sent = []
    for i in range(2):
        k = low + i
        begin = (2304 + 503 * k + 2560) // 256 - 10
        good = (me_b < 7) & (k >= 0) & (k < n_blk) & (begin <= unit)
        mine = (me_s == 0) & (me_b == k)
        at = jnp.clip(unit - begin, 0, 2)
        away = pltpu.make_async_remote_copy(
            src_ref=unit_ref, dst_ref=uland.at[at, me_s], send_sem=usend.at[i],
            recv_sem=urecv.at[at], device_id=(0, jnp.clip(k, 0, n_blk - 1)), device_id_type=MESH,
        )
        home = pltpu.make_async_copy(unit_ref, uland.at[at, me_s], urecv.at[at])
        pl.when(good & mine)(home.start)
        pl.when(good & jnp.logical_not(mine))(away.start)
        sent.append((good & jnp.logical_not(mine), away))

    yrow[...] = dot(dot(lifted, w_up[...]).astype(BF16), perm_t[...])

    def fine_up(g, carry):
        spreadv = expand(g).reshape(4, CH, VOX)
        for bb in range(4):
            b = 4 * g + bb
            fine_out[b] = (mid[b].astype(F32) + spreadv[bb]).astype(BF16)
        return carry

    lax.fori_loop(0, NB // 4, fine_up, 0)
    store_out = pltpu.make_async_copy(fine_out, fine_out_hbm, osem.at[1])
    store_out.start()
    row_wait(wland, vrecv.at[0])
    gsum[...] = lax.fori_loop(
        1, n_blk, lambda i, c: c + wland[i].astype(F32), window_of(me_b)[...].astype(F32))

    my_unit = (16 * skew + 503 * me_b) // 256
    for u in range(3):
        @pl.when((me_s == 0) & (my_unit + u < 16))
        def _():
            pltpu.make_async_copy(uland.at[u], uland.at[u], urecv.at[u]).wait()
            rows = slice(16 * u, 16 * u + 16)
            gsum[rows, :] += jnp.sum(uland[u].astype(F32), axis=0)

    down_by = skew + 503 * me_b // 16 - 16 * my_unit
    left_by = 16 * (503 * me_b % 16)
    value = pltpu.roll(gsum[...], lax.rem(48 - down_by, 48), 0)
    value = pltpu.roll(value, lax.rem(WID - left_by, WID), 1)
    below = pltpu.roll(value, 47, 0)
    grads_out[...] = jnp.where(
        iota((32, WID), 1) < WID - left_by, value[:32], below[:32])

    for copy in copies1 + copies4 + copies2 + copies3 + x_sent + d_sent:
        copy.wait_send()
    pl.when(me_s != n_slab - 1)(up_sent.wait_send)
    pl.when(me_s != 0)(down_sent.wait_send)
    row_wait(pk_a, asend.at[0])
    row_wait(pk_b, asend.at[1])
    row_wait(rpk, asend.at[2])
    row_wait(wland, vsend)
    for t in range(7):
        pl.when(me_b != t)(fine_copies[t].wait_send)
    for good, copy in sent:
        pl.when(good)(copy.wait_send)
    store_grad.wait()
    store_out.wait()


def fused(n_slab, n_blk, *operands):
    vmem = pl.BlockSpec(memory_space=pltpu.VMEM)
    smem = pl.BlockSpec(memory_space=pltpu.SMEM)
    hbm = pl.BlockSpec(memory_space=pl.ANY)
    sds = jax.ShapeDtypeStruct
    fine_like = sds((NB, CH, VOX), BF16)
    cells = sds((CELLS, WID), BF16)
    dma = pltpu.SemaphoreType.DMA
    rows = (n_blk, 16, 128)
    bf = lambda *shape: pltpu.VMEM(shape, BF16)
    f32 = lambda *shape: pltpu.VMEM(shape, F32)
    return pl.pallas_call(
        functools.partial(kernel, n_slab, n_blk),
        name="window",
        out_shape=(fine_like, cells, fine_like, cells, sds((32, WID), F32)),
        in_specs=[hbm] * 2 + [vmem] * 3 + [hbm] * 3 + [smem] * 3 + [hbm] * 2 + [vmem] + [hbm] * 4,
        out_specs=(hbm, vmem, hbm, vmem, vmem),
        scratch_shapes=[
            bf(NB, CH, VOX), bf(NB, CH, VOX), bf(VOX, WID), bf(WID, VOX), bf(27 * WID, WID),
            bf(VOX, 6 * 128), bf(6 * 128, VOX), bf(VOX, VOX), bf(VOX, VOX), bf(VOX, VOX),
            bf(VOX, VOX),
            bf(NB, CH, VOX), bf(NB, CH, VOX), bf(SLOTS, CH, 128), bf(SLOTS, CH, 128),
            bf(6, CH, NB * 128), bf(2, 3, CH, 128), bf(2, 3, CH, 128), bf(6, CH, 128),
            bf(6, CH, 128), bf(2, CH, 128), bf(6, CH, NB * 128), bf(NB, CH, 6 * 128),
            bf(NB, 7 * CH, VOX), f32(NB, CH, VOX), bf(NB, CH, VOX), bf(NB, CH, VOX),
            f32(NB, CH, VOX), f32(CELLS, VOX), f32(CELLS, VOX), f32(CH, 7 * CH),
            bf(n_blk * 16, 128), bf(*rows), bf(*rows), bf(*rows), bf(*rows), bf(*rows), bf(*rows),
            bf(8, CELLS, WID), bf(8, CELLS, WID), bf(CELLS, WID), bf(CELLS, WID), f32(7 * CH, CH),
            bf(CELLS, 3 * WID), bf(CELLS, WID), bf(CELLS, 3 * WID), bf(CELLS, 3 * WID),
            bf(n_slab, CELLS, 3 * WID), bf(n_slab, CELLS, WID), bf(n_slab, CELLS, 3 * WID),
            bf(n_slab, CELLS, 3 * WID),
            f32(CELLS, WID), bf(3, WID, 128), bf(5 * WID, WID), bf(n_blk, 48, WID), bf(7, 16, WID),
            bf(n_blk, 16, WID), bf(16, WID), bf(3, n_slab, 16, WID), f32(48, WID),
            pltpu.VMEM((8, 128), jnp.int32), pltpu.SMEM((8, 128), jnp.int32),
            dma((11,)), dma, dma((2,)), dma((4,)), dma((4,)), dma((3,)), dma((3,)), dma((16,)),
            dma((16,)), dma((32,)), dma((4,)), dma, dma((2,)), dma((9,)), dma((3,)),
        ],
        compiler_params=pltpu.CompilerParams(
            collective_id=0, has_side_effects=True, vmem_limit_bytes=56 * 1024 * 1024
        ),
    )(*operands)


def finish_kernel(fine_in, grad_in, coarse_in, latent_in, flat_in, fine_to, grad_to, coarse_to,
                  latent_to, flat_to):
    fine_to[...] = fine_in[...]
    grad_to[...] = grad_in[...]
    coarse_to[...] = coarse_in[...]
    latent_to[...] = latent_in[...]
    for r in range(SHARD // WID):
        flat_to[WID * r : WID * r + WID] = flat_in[r, :]
    rest = SHARD % WID
    flat_to[SHARD - rest : SHARD] = flat_in[SHARD // WID, :rest]


def finish(fine_out, coarse_out, grad_fine, grad_latent, flat):
    blocks = pl.BlockSpec((4, CH, VOX), lambda i: (i, 0, 0))
    cells = pl.BlockSpec((CELLS, WID), lambda i: (0, 0))
    like = lambda a: jax.ShapeDtypeStruct(a.shape, a.dtype)
    fine_out, grad_fine, coarse_out, grad_latent, flat = pl.pallas_call(
        finish_kernel,
        name="finish",
        grid=(NB // 4,),
        out_shape=(like(fine_out), like(grad_fine), like(coarse_out), like(grad_latent),
                   jax.ShapeDtypeStruct((SHARD,), F32)),
        in_specs=[blocks, blocks, cells, cells, pl.BlockSpec((32, WID), lambda i: (0, 0))],
        out_specs=(blocks, blocks, cells, cells, pl.BlockSpec((SHARD,), lambda i: (0,))),
    )(fine_out, grad_fine, coarse_out, grad_latent, flat)
    return fine_out, coarse_out, grad_fine, grad_latent, flat


def shards(
    n_slab, n_blk,
    fine_in, latent, w_fine, w_down, w_coarse, w_up, neighbors, pool_owner, pool_cell, cot_fine,
    cot_coarse,
):
    outs = fused(
        n_slab, n_blk,
        fine_in, cot_fine, latent.reshape(CELLS, WID), cot_coarse.reshape(CELLS, WID),
        w_fine.T, w_down, w_up, w_coarse, neighbors.T, pool_owner.reshape(NB), pool_cell,
        *tables())
    fine_out, c_out, grad_fine, g_lat, weight_grads = finish(*outs)
    return (fine_out, c_out.reshape(latent.shape), grad_fine, g_lat.reshape(latent.shape),
            weight_grads)


def solution(mesh):
    n_slab, n_blk = mesh.shape["slab"], mesh.shape["blk"]
    return jax.shard_map(
        functools.partial(shards, n_slab, n_blk),
        mesh=mesh,
        in_specs=(
            P(("slab", "blk"), None, None), P("slab", "blk", None, None), P(), P(), P(), P(),
            P(("slab", "blk"), None), P(("slab", "blk"), None), P(("slab", "blk")),
            P(("slab", "blk"), None, None), P("slab", "blk", None, None),
        ),
        out_specs=(
            P(("slab", "blk"), None, None), P("slab", "blk", None, None),
            P(("slab", "blk"), None, None), P("slab", "blk", None, None), P(("slab", "blk")),
        ),
        check_vma=False,
    )
```

time: 108 us -> 80.4 us (0.74)
  local copies, waits for them, and re-layouts: 13.2 us -> 0 us
  Pallas kernels: 90.2 us -> 79.5 us
  other arithmetic: 2.97 us -> 0 us
    pallas_call x1, Pallas kernels: 90.2 us -> 76.2 us  [fused(): pl.pallas_call(functools.partial(kernel, n_slab, n_blk), name='window', o...]
    unnamed x7 -> x0, local copies, waits for them, and re-layouts: 10.4 us -> none
    pallas_call x0 -> x1, Pallas kernels: none -> 3.38 us  [finish(): pl.pallas_call(finish_kernel, name='finish', grid=(NB // 4,), out_shape=(...]
    pad x2 -> x0, local copies, waits for them, and re-layouts: 1.21 us -> none  [shards(): pad = lambda a: jnp.pad(a.reshape(NB, 1), ((0, CELLS - NB), (0, 0)))]
where the time goes in v2:
time: 80.4 us; the launch traced here: 80.2 us
  Pallas kernels  79.5 us (99%)
    pallas_call x1, Pallas kernels, fused(): pl.pallas_call(functools.partial(kernel, n_slab, n_blk), name='window', o...  76.2 us
    pallas_call x1, Pallas kernels, finish(): pl.pallas_call(finish_kernel, name='finish', grid=(NB // 4,), out_shape=(...  3.38 us

profile of v2, /device:TPU:32, one launch (start us, length us, event | category | flops | bytes accessed | tf_op | source)
XLA Modules:
  0.0 80.2 jit_solution(12638340252980663843)
XLA Ops:
  0.6 76.2 %window.1 = (bf16[12,64,512]{2,1,0:T(8,128)(2,1)}, bf16[16,256]{1,0:T(8,128)(2,1)}, bf16[12,64,512]{2,1,0:T(8,128)(2,1)}, bf16[16,256]{1,0:T(8,128)(2,1)}, f32[32,256]{1,0:T(8,128)}) custom-call(bf16[12,64,512]{2,1,0:T(8,128)(2,1)} %fine_hbm.1, bf16[12,64,512]{2,1,0:T(8,128)(2,1)} %cot_hbm.1, bf16[16,256]{1,0:T(8,128)(2,1)} %bitcast.8, ...), custom_call_target="tpu_custom_call" | custom-call | tf_op jit(solution)/shard_map/window/pallas_call | solution.py:670
  76.8 3.4 %finish.1 = (bf16[12,64,512]{2,1,0:T(8,128)(2,1)}, bf16[12,64,512]{2,1,0:T(8,128)(2,1)}, bf16[16,256]{1,0:T(8,128)(2,1)}, bf16[16,256]{1,0:T(8,128)(2,1)}, f32[8048]{0:T(1024)}) custom-call(bf16[12,64,512]{2,1,0:T(8,128)(2,1)} %get-tuple-element.15.fine_in, bf16[12,64,512]{2,1,0:T(8,128)(2,1)} %get-tuple-element.16.grad_in, ...), custom_call_target="tpu_custom_call" | custom-call | tf_op jit(solution)/shard_map/finish/pallas_call | solution.py:718

commit v3 on v2

--- a/solution.py
+++ b/solution.py
@@ -23,6 +23,8 @@
 ZERO = FACES + 6
 SLOTS = FACES + 7
 OFFSETS = ((-1, -1), (-1, 0), (-1, 1), (0, -1), (0, 1), (1, -1), (1, 0), (1, 1))
+WIDE = tuple((a, b) for a in range(-2, 3) for b in range(-2, 3) if (a, b) != (0, 0))
+BOXES = tuple((a, b) for a in range(-1, 2) for b in range(-1, 2))
 SHARD = 8048
 SLAB_ROWS = 1006
 MESH = pl.DeviceIdType.MESH
@@ -77,9 +79,9 @@
     pull_hbm, place_hbm, keep, spread_hbm, spread_t_hbm, perm_hbm, perm_t_hbm,
     fine_out_hbm, coarse_out, grad_fine_hbm, grad_latent, grads_out,
     fine, cot, w_down, w_up, w_coarse, pull, place, spread, spread_t, perm, perm_t,
-    fine_out, grad_fine, faces1, faces2, faces_wide, pack1, pack2, land1, land2, half, near, zall,
-    taps, pre, mid, dpf, big, ysum, yrow, w_bwd, route_pk, arr_a, arr_b, pk_a, pk_b, rpk, rarr,
-    rim1, rim2, rimsrc1, rimsrc2, gacc, xsrc, dsrc, upsrc, downsrc, xgat, dgat, upgat, downgat,
+    fine_out, grad_fine, faces1, faces2, faces_wide, pack1, pack2, land1, land2, half, near1, near2, zall,
+    own_taps, back_taps, pre, mid, dpf, big, ysum, yrow, w_bwd, route_pk, arr_a, arr_b, pk_a, pk_b, rpk, rarr,
+    rim1, rim2, rimsrc1, rimsrc2, triple, boxes, d_box, d_all, gacc, xsrc, dsrc, upsrc, downsrc, xgat, dgat, upgat, downgat,
     dco, xq, gbuf, wland, fsrc, fland, unit_ref, uland, gsum, idx_v, idx_s,
     wsem, isem, osem, fsend, frecv, asend, arecv, rsend, rrecv, csend, crecv, vsend, vrecv,
     usend, urecv,
@@ -114,7 +116,7 @@
     lax.fori_loop(1, n_blk, greet, 0)
     for i in range(1, n_slab):
         pl.semaphore_signal(barrier, inc=1, device_id=column(i), device_id_type=MESH)
-    for a, b in OFFSETS:
+    for a, b in WIDE:
         if a != 0 and b != 0:
             pl.semaphore_signal(barrier, inc=1, device_id=near_id(a, b), device_id_type=MESH)
     for k in (before, after):
@@ -192,16 +194,16 @@
             ),
         ]
 
-    def roll_taps(src, b):
+    def roll_taps(src, b, taps, at):
         x = src[b]
         wide = x.astype(F32)
-        taps[b, 0:CH, :] = x
+        taps[at, 0:CH, :] = x
         for d in range(6):
             stride = STRIDES[d // 2]
             moved = pltpu.roll(wide, stride if d % 2 == 0 else VOX - stride, 1)
-            taps[b, CH * (d + 1) : CH * (d + 2), :] = (moved * keep[d]).astype(BF16)
-
-    def gather_faces(faces, land):
+            taps[at, CH * (d + 1) : CH * (d + 2), :] = (moved * keep[d]).astype(BF16)
+
+    def gather_faces(faces, land, near):
         faces[PREV0 : PREV0 + 6] = land[...]
         for d in range(6):
             for b in range(NB):
@@ -209,7 +211,7 @@
                 near[d, :, 128 * b : 128 * b + 128] = (
                     faces[lax.shift_right_logical(at, 1)] * half[lax.bitwise_and(at, 1)])
 
-    def weigh_faces(w):
+    def weigh_faces(w, near):
         for d in range(6):
             z = dot(w[:, CH * (d + 1) : CH * (d + 2)], near[d]).astype(BF16)
             for b in range(NB):
@@ -234,8 +236,8 @@
             parts.append((row * eye).astype(BF16))
         return dot(jnp.concatenate(parts, axis=0), spread_t[...])
 
-    def row_wait(buf, sem):
-        pltpu.make_async_copy(buf.at[pl.ds(1, n_blk - 1)], buf.at[pl.ds(1, n_blk - 1)], sem).wait()
+    def row_wait(buf, sem, count=n_blk - 1):
+        pltpu.make_async_copy(buf.at[pl.ds(1, count)], buf.at[pl.ds(1, count)], sem).wait()
 
     def send_rows(src, dst, back, k):
         def body(i, carry):
@@ -249,10 +251,10 @@
 
     loads["fine"].wait()
     loads["pull"].wait()
-    make_faces(fine, faces1, faces_wide)
+    make_faces(fine, faces1, None)
     load_idx.wait()
     make_packs(faces1, pack1)
-    pl.semaphore_wait(barrier, n_blk - 1 + n_slab - 1 + 4 + 2)
+    pl.semaphore_wait(barrier, n_blk - 1 + n_slab - 1 + 16 + 2)
     copies1 = face_copies(land1, pack1, 0)
     for copy in copies1:
         copy.start()
@@ -298,16 +300,16 @@
         w_bwd[:, CH * e : CH * e + CH] = w_fwd[:, CH * d : CH * d + CH].astype(F32).T
 
     def own_forward(b, carry):
-        roll_taps(fine, b)
-        pre[b] = dot(w_fwd[...], taps[b])
+        roll_taps(fine, b, own_taps, b)
+        pre[b] = dot(w_fwd[...], own_taps[b])
         return carry
 
     lax.fori_loop(0, NB, own_forward, 0)
     loads["place"].wait()
     for copy in copies1:
         copy.wait_recv()
-    gather_faces(faces1, land1)
-    weigh_faces(w_fwd[...])
+    gather_faces(faces1, land1, near1)
+    weigh_faces(w_fwd[...], near1)
 
     def fine_forward(g, carry):
         more = placed(g).reshape(4, CH, VOX)
@@ -344,27 +346,30 @@
     dco[...] = cotc[...].astype(F32) + lift[:CELLS] + lift[CELLS:]
     loads["down"].wait()
 
+    def rim_copies(src, dst, offsets, base):
+        count = len(offsets)
+        return [
+            pltpu.make_async_remote_copy(
+                src_ref=src, dst_ref=dst.at[count - 1 - i], send_sem=rsend.at[base + i],
+                recv_sem=rrecv.at[base + count - 1 - i], device_id=near_id(a, b),
+                device_id_type=MESH,
+            )
+            for i, (a, b) in enumerate(offsets)
+        ]
+
+    def inside(a, b):
+        zz, yy = me_s + a, me_b + b
+        within = (zz >= 0) & (zz < n_slab) & (yy >= 0) & (yy < n_blk)
+        return jnp.where(within, 1.0, 0.0)
+
+    rimsrc2[...] = dco[...]
+    copies3 = rim_copies(rimsrc2, rim2, OFFSETS, len(WIDE))
+    for copy in copies3:
+        copy.start()
     row_wait(arr_b, arecv.at[1])
     means_hi, means_lo = two_parts(dot(hot_t, lined(arr_b)))
     pooled = dot(jnp.concatenate([means_hi, means_lo], axis=0), w_down[...])
     c_in = (latent[...].astype(F32) + pooled[:CELLS] + pooled[CELLS:]).astype(BF16)
-
-    def rim_copies(src, dst, k):
-        return [
-            pltpu.make_async_remote_copy(
-                src_ref=src, dst_ref=dst.at[7 - i], send_sem=rsend.at[8 * k + i],
-                recv_sem=rrecv.at[8 * k + 7 - i], device_id=near_id(a, b), device_id_type=MESH,
-            )
-            for i, (a, b) in enumerate(OFFSETS)
-        ]
-
-    def rim_tile(dst, own, a, b):
-        if a == 0 and b == 0:
-            return own.astype(F32)
-        zz, yy = me_s + a, me_b + b
-        inside = (zz >= 0) & (zz < n_slab) & (yy >= 0) & (yy < n_blk)
-        tile = dst[OFFSETS.index((a, b))].astype(F32)
-        return tile * jnp.where(inside, 1.0, 0.0)
 
     sub_x = iota((CELLS, WID), 0)
 
@@ -387,50 +392,74 @@
             copy.start()
         return made
 
-    def plane_copy(src, dst, slab, k):
-        copy = pltpu.make_async_remote_copy(
-            src_ref=src, dst_ref=dst.at[me_s], send_sem=csend.at[8 * k], recv_sem=crecv.at[k],
-            device_id=(slab, me_b), device_id_type=MESH,
-        )
-        pl.when(me_s != slab)(copy.start)
-        pl.when(me_s == slab)(pltpu.make_async_copy(src, dst.at[me_s], crecv.at[k]).start)
-        return copy
+    odd = lax.rem(me_b, 2)
+    even_row = me_b - odd
+
+    def plane_copies(src, dst, slab, k):
+        made = []
+        for i in range(2):
+            k_blk = even_row + i
+            copy = pltpu.make_async_remote_copy(
+                src_ref=src, dst_ref=dst.at[odd, me_s], send_sem=csend.at[8 * k + i],
+                recv_sem=crecv.at[k], device_id=(slab, k_blk), device_id_type=MESH,
+            )
+            mine = (me_s == slab) & (me_b == k_blk)
+            pl.when(jnp.logical_not(mine))(copy.start)
+            pl.when(mine)(pltpu.make_async_copy(src, dst.at[odd, me_s], crecv.at[k]).start)
+            made.append((jnp.logical_not(mine), copy))
+        return made
 
     rimsrc1[...] = c_in
-    copies2 = rim_copies(rimsrc1, rim1, 0)
+    copies2 = rim_copies(rimsrc1, rim1, WIDE, 0)
     for copy in copies2:
         copy.start()
     loads["coarse"].wait()
     for copy in copies2:
         copy.wait_recv()
+
+    for a in range(-2, 3):
+        for b in range(-2, 3):
+            if a == 0 and b == 0:
+                tile = c_in.astype(F32)
+            else:
+                tile = rim1[WIDE.index((a, b))].astype(F32) * inside(a, b)
+            triple[5 * (a + 2) + b + 2] = jnp.concatenate(
+                [along_x(tile, r - 1) for r in range(3)], axis=1).astype(BF16)
+    plane_row = lambda b: triple[12 + b, :, WID : 2 * WID]
     xsrc[...] = jnp.concatenate(
-        [rim_tile(rim1, c_in, 0, q - 1) for q in range(3)], axis=1).astype(BF16)
+        [jnp.where(odd == 0, plane_row(i - 1).astype(F32), plane_row(i - 2).astype(F32))
+         for i in range(4)], axis=1).astype(BF16)
     x_sent = column_copies(xsrc, xgat, 0)
+    acc = jnp.zeros((9 * CELLS, WID), F32)
+    for p in range(3):
+        for q in range(3):
+            rows = jnp.concatenate(
+                [triple[5 * (a + p + 1) + b + q + 1] for a, b in BOXES], axis=0)
+            base = (p * 3 + q) * 3 * WID
+            acc = acc + dot(rows, w_coarse[base : base + 3 * WID, :])
+    boxes[...] = acc
+    for copy in copies3:
+        copy.wait_recv()
+    for i, (a, b) in enumerate(BOXES):
+        value = boxes[CELLS * i : CELLS * i + CELLS]
+        sig = jax.nn.sigmoid(value)
+        slope = sig * (1.0 + value * (1.0 - sig))
+        if i == 4:
+            d_pre = dco[...] * slope
+            c_out = (c_in.astype(F32) + value * sig).astype(BF16)
+        else:
+            d_pre = rim2[OFFSETS.index((a, b))] * slope * inside(a, b)
+        d_box[i] = d_pre.astype(BF16).astype(F32)
+    coarse_out[...] = c_out
+    dsrc[...] = jnp.concatenate(
+        [jnp.where(odd == 0, d_box[4 + i], d_box[3 + i]) for i in range(2)], axis=1).astype(BF16)
+    d_sent = column_copies(dsrc, dgat, 1)
+    upsrc[...] = jnp.concatenate([c_out.astype(F32), raised_hi.astype(F32)], axis=1).astype(BF16)
+    up_sent = plane_copies(upsrc, upgat, n_slab - 1, 2)
     acc = jnp.zeros((CELLS, WID), F32)
     for p in range(3):
         for q in range(3):
-            tile = rim_tile(rim1, c_in, p - 1, q - 1)
-            row = jnp.concatenate([along_x(tile, r - 1) for r in range(3)], axis=1).astype(BF16)
-            base = (p * 3 + q) * 3 * WID
-            acc = acc + dot(row, w_coarse[base : base + 3 * WID, :])
-    sig = jax.nn.sigmoid(acc)
-    d_pre = (dco[...] * (sig * (1.0 + acc * (1.0 - sig)))).astype(BF16)
-    rimsrc2[...] = d_pre
-    copies3 = rim_copies(rimsrc2, rim2, 1)
-    for copy in copies3:
-        copy.start()
-    c_out = (c_in.astype(F32) + acc * sig).astype(BF16)
-    coarse_out[...] = c_out
-    dsrc[...] = d_pre
-    d_sent = column_copies(dsrc, dgat, 1)
-    upsrc[...] = jnp.concatenate([c_out.astype(F32), raised_hi.astype(F32)], axis=1).astype(BF16)
-    up_sent = plane_copy(upsrc, upgat, n_slab - 1, 2)
-    for copy in copies3:
-        copy.wait_recv()
-    acc = jnp.zeros((CELLS, WID), F32)
-    for p in range(3):
-        for q in range(3):
-            tile = rim_tile(rim2, d_pre, 1 - p, 1 - q)
+            tile = d_box[3 * (2 - p) + 2 - q]
             for r in range(3):
                 base = ((p * 3 + q) * 3 + r) * WID
                 moved = along_x(tile, 1 - r).astype(BF16)
@@ -448,27 +477,28 @@
     rarr[0] = rpk[0]
     send_rows(rpk, rarr, True, 2)
     downsrc[...] = jnp.concatenate([g_lat.astype(F32), means_hi.astype(F32)], axis=1).astype(BF16)
-    down_sent = plane_copy(downsrc, downgat, 0, 3)
+    down_sent = plane_copies(downsrc, downgat, 0, 3)
 
     base_row = me_s * SLAB_ROWS + 144
     first_tap = base_row // WID - 3
     skew = base_row % WID
     pltpu.make_async_copy(xgat, xgat, crecv.at[0]).wait()
-    everything = xgat[...].reshape(n_slab * CELLS, 3 * WID).astype(F32)
-    for q in range(3):
+    everything = xgat[...].reshape(n_slab * CELLS, 4 * WID).astype(F32)
+    for q in range(4):
         xq[q] = everything[:, q * WID : q * WID + WID].T.astype(BF16)
     pltpu.make_async_copy(dgat, dgat, crecv.at[1]).wait()
-    d_all = dgat[...].reshape(n_slab * CELLS, WID)
+    pair = dgat[...].reshape(n_slab * CELLS, 2 * WID)
+    d_all[...] = jnp.concatenate([pair[:, :WID], pair[:, WID:]], axis=0)
 
     def tap_rows(i, carry):
         t = first_tap + i
-        inside = (t >= 0) & (t < 27)
+        good = (t >= 0) & (t < 27)
         tc = jnp.clip(t, 0, 26)
         p, q, r = tc // 9, tc // 3 % 3, tc % 3
-        shift = (sub // 16 == lane // 16 + p - 1) & (sub % 16 == lane % 16 + r - 1)
-        moved = dot(xq[q], shift.astype(BF16)).astype(BF16)
+        shift = ((sub // 16 == lane // 16 + p - 1) & (sub % 16 == lane % 16 + r - 1)).astype(BF16)
+        moved = jnp.concatenate([dot(xq[q], shift), dot(xq[q + 1], shift)], axis=1).astype(BF16)
         gbuf[pl.ds(pl.multiple_of(i * WID, WID), WID), :] = (
-            dot(moved, d_all) * jnp.where(inside, 1.0 / math.sqrt(CELLS * total), 0.0)
+            dot(moved, d_all[...]) * jnp.where(good, 1.0 / math.sqrt(CELLS * total), 0.0)
         ).astype(BF16)
         return carry
 
@@ -478,10 +508,10 @@
     @pl.when(me_s == n_slab - 1)
     def _():
         pltpu.make_async_copy(upgat, upgat, crecv.at[2]).wait()
-        left = upgat[:, :, :WID].reshape(n_slab * CELLS, WID)
+        left = upgat[:, :, :, :WID].reshape(2 * n_slab * CELLS, WID)
         twice = (iota((WID, VOX), 1) // 2 == iota((WID, VOX), 0)).astype(BF16)
         left = dot(left, twice).astype(BF16)
-        right = upgat[:, :, WID:].reshape(n_slab * CELLS, VOX)
+        right = upgat[:, :, :, WID:].reshape(2 * n_slab * CELLS, VOX)
         up = jnp.where(iota((VOX, WID), 0) % 2 == 0, dot_tn(left, right[:, :WID]),
                        dot_tn(left, right[:, WID:]))
         gbuf[512:1024, :] = (up * rows_scale).astype(BF16)
@@ -489,8 +519,8 @@
     @pl.when(me_s == 0)
     def _():
         pltpu.make_async_copy(downgat, downgat, crecv.at[3]).wait()
-        left = downgat[:, :, WID:].reshape(n_slab * CELLS, VOX)
-        right = downgat[:, :, :WID].reshape(n_slab * CELLS, WID)
+        left = downgat[:, :, :, WID:].reshape(2 * n_slab * CELLS, VOX)
+        right = downgat[:, :, :, :WID].reshape(2 * n_slab * CELLS, WID)
         gbuf[256:768, :] = (dot_tn(left, right) * rows_scale).astype(BF16)
 
     def window_of(k):
@@ -499,12 +529,12 @@
 
     def send_window(i, carry):
         pltpu.make_async_remote_copy(
-            src_ref=window_of(lax.rem(me_b + i, n_blk)), dst_ref=wland.at[i],
-            send_sem=vsend, recv_sem=vrecv.at[0], device_id=rel(i), device_id_type=MESH,
+            src_ref=window_of(lax.rem(me_b + 2 * i, n_blk)), dst_ref=wland.at[i],
+            send_sem=vsend, recv_sem=vrecv.at[0], device_id=rel(2 * i), device_id_type=MESH,
         ).start()
         return carry
 
-    lax.fori_loop(1, n_blk, send_window, 0)
+    lax.fori_loop(1, n_blk // 2, send_window, 0)
     loads["perm_t"].wait()
     loads["spread_t"].wait()
     row_wait(rarr, arecv.at[2])
@@ -527,7 +557,7 @@
         return carry
 
     lax.fori_loop(0, NB // 4, fine_slope, 0)
-    make_faces(dpf, faces2, None)
+    make_faces(dpf, faces2, faces_wide)
     make_packs(faces2, pack2)
     copies4 = face_copies(land2, pack2, 1)
     for copy in copies4:
@@ -535,28 +565,20 @@
     w_back = w_bwd[...].astype(BF16)
     gacc[...] = jnp.zeros((7 * CH, CH), F32)
 
-    def own_backward(b, carry):
-        roll_taps(dpf, b)
-        t = taps[b]
-        big[b] += dot(w_back, t)
-        gacc[...] += dot_nt(t, fine[b])
-        return carry
-
-    lax.fori_loop(0, NB, own_backward, 0)
-    for copy in copies4:
-        copy.wait_recv()
-    gather_faces(faces2, land2)
-    for e in range(6):
-        gacc[CH * (e + 1) : CH * (e + 2), :] += dot_nt(near[e], faces_wide[e])
+    def weight_grad(b, carry):
+        gacc[...] += dot_nt(own_taps[b], dpf[b])
+        return carry
+
+    lax.fori_loop(0, NB, weight_grad, 0)
+    for d in range(6):
+        gacc[CH * (d + 1) : CH * (d + 2), :] += dot_nt(near1[d], faces_wide[d])
     fine_bf = (gacc[...] * (1.0 / math.sqrt(NB * total * VOX))).astype(BF16)
+    row_to = iota((7 * 16, 7 * CH), 0)
     quarters = []
     for m in range(4):
-        pick = (iota((16, CH), 1) == 4 * iota((16, CH), 0) + m).astype(BF16)
-        quarters.append(dot_nt(pick, fine_bf))
-    for e in range(7):
-        d = 0 if e == 0 else OPPOSITE[e - 1] + 1
-        fsrc[d] = jnp.concatenate(
-            [quarter[:, CH * e : CH * e + CH] for quarter in quarters], axis=1).astype(BF16)
+        pick = iota((7 * 16, 7 * CH), 1) == 64 * (row_to // 16) + 4 * (row_to % 16) + m
+        quarters.append(dot(pick.astype(BF16), fine_bf))
+    fsrc[...] = jnp.concatenate(quarters, axis=1).astype(BF16).reshape(7, 16, WID)
     fine_copies = [
         pltpu.make_async_remote_copy(
             src_ref=fsrc.at[t], dst_ref=fland.at[me_b], send_sem=usend.at[2 + t],
@@ -571,7 +593,17 @@
     def _():
         pltpu.make_async_copy(fsrc.at[lax.rem(me_b, 7)], fland.at[me_b], vrecv.at[1]).start()
 
-    weigh_faces(w_back)
+    def own_backward(b, carry):
+        buf = lax.rem(b, 2)
+        roll_taps(dpf, b, back_taps, buf)
+        big[b] += dot(w_back, back_taps[buf])
+        return carry
+
+    lax.fori_loop(0, NB, own_backward, 0)
+    for copy in copies4:
+        copy.wait_recv()
+    gather_faces(faces2, land2, near2)
+    weigh_faces(w_back, near2)
 
     def fine_backward(g, carry):
         more = placed(g).reshape(4, CH, VOX)
@@ -620,9 +652,9 @@
     lax.fori_loop(0, NB // 4, fine_up, 0)
     store_out = pltpu.make_async_copy(fine_out, fine_out_hbm, osem.at[1])
     store_out.start()
-    row_wait(wland, vrecv.at[0])
+    row_wait(wland, vrecv.at[0], n_blk // 2 - 1)
     gsum[...] = lax.fori_loop(
-        1, n_blk, lambda i, c: c + wland[i].astype(F32), window_of(me_b)[...].astype(F32))
+        1, n_blk // 2, lambda i, c: c + wland[i].astype(F32), window_of(me_b)[...].astype(F32))
 
     my_unit = (16 * skew + 503 * me_b) // 256
     for u in range(3):
@@ -642,12 +674,12 @@
 
     for copy in copies1 + copies4 + copies2 + copies3 + x_sent + d_sent:
         copy.wait_send()
-    pl.when(me_s != n_slab - 1)(up_sent.wait_send)
-    pl.when(me_s != 0)(down_sent.wait_send)
+    for good, copy in up_sent + down_sent:
+        pl.when(good)(copy.wait_send)
     row_wait(pk_a, asend.at[0])
     row_wait(pk_b, asend.at[1])
     row_wait(rpk, asend.at[2])
-    row_wait(wland, vsend)
+    row_wait(wland, vsend, n_blk // 2 - 1)
     for t in range(7):
         pl.when(me_b != t)(fine_copies[t].wait_send)
     for good, copy in sent:
@@ -679,19 +711,21 @@
             bf(VOX, VOX),
             bf(NB, CH, VOX), bf(NB, CH, VOX), bf(SLOTS, CH, 128), bf(SLOTS, CH, 128),
             bf(6, CH, NB * 128), bf(2, 3, CH, 128), bf(2, 3, CH, 128), bf(6, CH, 128),
-            bf(6, CH, 128), bf(2, CH, 128), bf(6, CH, NB * 128), bf(NB, CH, 6 * 128),
-            bf(NB, 7 * CH, VOX), f32(NB, CH, VOX), bf(NB, CH, VOX), bf(NB, CH, VOX),
+            bf(6, CH, 128), bf(2, CH, 128), bf(6, CH, NB * 128), bf(6, CH, NB * 128),
+            bf(NB, CH, 6 * 128), bf(NB, 7 * CH, VOX), bf(2, 7 * CH, VOX), f32(NB, CH, VOX), bf(NB, CH, VOX), bf(NB, CH, VOX),
             f32(NB, CH, VOX), f32(CELLS, VOX), f32(CELLS, VOX), f32(CH, 7 * CH),
             bf(n_blk * 16, 128), bf(*rows), bf(*rows), bf(*rows), bf(*rows), bf(*rows), bf(*rows),
-            bf(8, CELLS, WID), bf(8, CELLS, WID), bf(CELLS, WID), bf(CELLS, WID), f32(7 * CH, CH),
-            bf(CELLS, 3 * WID), bf(CELLS, WID), bf(CELLS, 3 * WID), bf(CELLS, 3 * WID),
-            bf(n_slab, CELLS, 3 * WID), bf(n_slab, CELLS, WID), bf(n_slab, CELLS, 3 * WID),
-            bf(n_slab, CELLS, 3 * WID),
-            f32(CELLS, WID), bf(3, WID, 128), bf(5 * WID, WID), bf(n_blk, 48, WID), bf(7, 16, WID),
+            bf(24, CELLS, WID), f32(8, CELLS, WID), bf(CELLS, WID), f32(CELLS, WID),
+            bf(25, CELLS, 3 * WID), f32(9 * CELLS, WID), f32(9, CELLS, WID), bf(WID, WID),
+            f32(7 * CH, CH),
+            bf(CELLS, 4 * WID), bf(CELLS, 2 * WID), bf(CELLS, 3 * WID), bf(CELLS, 3 * WID),
+            bf(n_slab, CELLS, 4 * WID), bf(n_slab, CELLS, 2 * WID), bf(2, n_slab, CELLS, 3 * WID),
+            bf(2, n_slab, CELLS, 3 * WID),
+            f32(CELLS, WID), bf(4, WID, 128), bf(5 * WID, WID), bf(n_blk // 2, 48, WID), bf(7, 16, WID),
             bf(n_blk, 16, WID), bf(16, WID), bf(3, n_slab, 16, WID), f32(48, WID),
             pltpu.VMEM((8, 128), jnp.int32), pltpu.SMEM((8, 128), jnp.int32),
-            dma((11,)), dma, dma((2,)), dma((4,)), dma((4,)), dma((3,)), dma((3,)), dma((16,)),
-            dma((16,)), dma((32,)), dma((4,)), dma, dma((2,)), dma((9,)), dma((3,)),
+            dma((11,)), dma, dma((2,)), dma((4,)), dma((4,)), dma((3,)), dma((3,)), dma((32,)),
+            dma((32,)), dma((32,)), dma((4,)), dma, dma((2,)), dma((9,)), dma((3,)),
         ],
         compiler_params=pltpu.CompilerParams(
             collective_id=0, has_side_effects=True, vmem_limit_bytes=56 * 1024 * 1024
@@ -700,29 +734,42 @@
 
 
 def finish_kernel(fine_in, grad_in, coarse_in, latent_in, flat_in, fine_to, grad_to, coarse_to,
-                  latent_to, flat_to):
-    fine_to[...] = fine_in[...]
-    grad_to[...] = grad_in[...]
+                  latent_to, flat_to, held, in_sems, out_sems):
+    takes, gives = [], []
+    for i, (src, dst) in enumerate(((fine_in, fine_to), (grad_in, grad_to))):
+        for j in range(4):
+            rows = pl.ds(3 * j, 3)
+            n = 4 * i + j
+            takes.append(pltpu.make_async_copy(src.at[rows], held.at[i, rows], in_sems.at[n]))
+            gives.append(pltpu.make_async_copy(held.at[i, rows], dst.at[rows], out_sems.at[n]))
+    for copy in takes:
+        copy.start()
     coarse_to[...] = coarse_in[...]
     latent_to[...] = latent_in[...]
     for r in range(SHARD // WID):
         flat_to[WID * r : WID * r + WID] = flat_in[r, :]
     rest = SHARD % WID
     flat_to[SHARD - rest : SHARD] = flat_in[SHARD // WID, :rest]
+    for take, give in zip(takes, gives):
+        take.wait()
+        give.start()
+    for give in gives:
+        give.wait()
 
 
 def finish(fine_out, coarse_out, grad_fine, grad_latent, flat):
-    blocks = pl.BlockSpec((4, CH, VOX), lambda i: (i, 0, 0))
-    cells = pl.BlockSpec((CELLS, WID), lambda i: (0, 0))
+    hbm = pl.BlockSpec(memory_space=pl.ANY)
+    vmem = pl.BlockSpec(memory_space=pltpu.VMEM)
     like = lambda a: jax.ShapeDtypeStruct(a.shape, a.dtype)
     fine_out, grad_fine, coarse_out, grad_latent, flat = pl.pallas_call(
         finish_kernel,
         name="finish",
-        grid=(NB // 4,),
         out_shape=(like(fine_out), like(grad_fine), like(coarse_out), like(grad_latent),
                    jax.ShapeDtypeStruct((SHARD,), F32)),
-        in_specs=[blocks, blocks, cells, cells, pl.BlockSpec((32, WID), lambda i: (0, 0))],
-        out_specs=(blocks, blocks, cells, cells, pl.BlockSpec((SHARD,), lambda i: (0,))),
+        in_specs=[hbm, hbm, vmem, vmem, vmem],
+        out_specs=(hbm, hbm, vmem, vmem, vmem),
+        scratch_shapes=[pltpu.VMEM((2, NB, CH, VOX), BF16), pltpu.SemaphoreType.DMA((8,)),
+                        pltpu.SemaphoreType.DMA((8,))],
     )(fine_out, grad_fine, coarse_out, grad_latent, flat)
     return fine_out, coarse_out, grad_fine, grad_latent, flat
 

time: 80.4 us -> 69.5 us (0.86)
  Pallas kernels: 79.5 us -> 68.4 us
    pallas_call x1, Pallas kernels: 76.2 us -> 64.7 us  [fused(): pl.pallas_call(functools.partial(kernel, n_slab, n_blk), name='window', o...]
where the time goes in v3:
time: 69.5 us; the launch traced here: 69 us
  Pallas kernels  68.4 us (98%)
    pallas_call x1, Pallas kernels, fused(): pl.pallas_call(functools.partial(kernel, n_slab, n_blk), name='window', o...  64.7 us
    pallas_call x1, Pallas kernels, finish(): pl.pallas_call(finish_kernel, name='finish', out_shape=(like(fine_out), l...  3.7 us

profile of v3, /device:TPU:32, one launch (start us, length us, event | category | flops | bytes accessed | tf_op | source)
XLA Modules:
  0.0 69.0 jit_solution(5185474932152531622)
XLA Ops:
  0.6 64.7 %window.1 = (bf16[12,64,512]{2,1,0:T(8,128)(2,1)}, bf16[16,256]{1,0:T(8,128)(2,1)}, bf16[12,64,512]{2,1,0:T(8,128)(2,1)}, bf16[16,256]{1,0:T(8,128)(2,1)}, f32[32,256]{1,0:T(8,128)}) custom-call(bf16[12,64,512]{2,1,0:T(8,128)(2,1)} %fine_hbm.1, bf16[12,64,512]{2,1,0:T(8,128)(2,1)} %cot_hbm.1, bf16[16,256]{1,0:T(8,128)(2,1)} %bitcast.8, ...), custom_call_target="tpu_custom_call" | custom-call | tf_op jit(solution)/shard_map/window/pallas_call | solution.py:702
  65.3 3.7 %finish.1 = (bf16[12,64,512]{2,1,0:T(8,128)(2,1)}, bf16[12,64,512]{2,1,0:T(8,128)(2,1)}, bf16[16,256]{1,0:T(8,128)(2,1)}, bf16[16,256]{1,0:T(8,128)(2,1)}, f32[8048]{0:T(1024)}) custom-call(bf16[12,64,512]{2,1,0:T(8,128)(2,1)} %get-tuple-element.15.fine_in, bf16[12,64,512]{2,1,0:T(8,128)(2,1)} %get-tuple-element.16.grad_in, ...), custom_call_target="tpu_custom_call" | custom-call | tf_op jit(solution)/shard_map/finish/pallas_call | solution.py:764

commit v4 on v3

--- a/solution.py
+++ b/solution.py
@@ -26,6 +26,7 @@
 WIDE = tuple((a, b) for a in range(-2, 3) for b in range(-2, 3) if (a, b) != (0, 0))
 BOXES = tuple((a, b) for a in range(-1, 2) for b in range(-1, 2))
 SHARD = 8048
+FAR_FIRST = sorted(range(1, 32), key=lambda i: -(min(i // 8, 4 - i // 8) + min(i % 8, 8 - i % 8)))
 SLAB_ROWS = 1006
 MESH = pl.DeviceIdType.MESH
 F32 = jnp.float32
@@ -93,19 +94,31 @@
     after = lax.rem(pos + 1, total)
     before = lax.rem(pos + total - 1, total)
     rel = lambda i: (me_s, lax.rem(me_b + i, n_blk))
+    me_x, me_z = lax.div(me_b, 8), lax.rem(me_b, 8)
+    apart = lambda dx, dz: (me_s, lax.rem(me_x + dx, 4) * 8 + lax.rem(me_z + dz, 8))
     column = lambda i: (lax.rem(me_s + i, n_slab), me_b)
     flat = lambda k: (lax.div(k, n_blk), lax.rem(k, n_blk))
     near_id = lambda a, b: (lax.rem(me_s + a + n_slab, n_slab), lax.rem(me_b + b + n_blk, n_blk))
 
     loads = {}
-    for i, (name, src, dst) in enumerate((
-        ("fine", fine_hbm, fine), ("pull", pull_hbm, pull), ("cot", cot_hbm, cot),
-        ("spread", spread_hbm, spread), ("perm", perm_hbm, perm), ("place", place_hbm, place),
-        ("up", w_up_hbm, w_up), ("down", w_down_hbm, w_down), ("coarse", w_coarse_hbm, w_coarse),
-        ("perm_t", perm_t_hbm, perm_t), ("spread_t", spread_t_hbm, spread_t),
-    )):
-        loads[name] = pltpu.make_async_copy(src, dst, wsem.at[i])
-        loads[name].start()
+
+    def load(name, src, dst, parts=1):
+        size = src.shape[0] // parts
+        loads[name] = []
+        for i in range(parts):
+            rows = pl.ds(size * i, size)
+            copy = pltpu.make_async_copy(src.at[rows], dst.at[rows], wsem.at[len(taken)])
+            taken.append(name)
+            loads[name].append(copy)
+            copy.start()
+
+    def loaded(name):
+        for copy in loads[name]:
+            copy.wait()
+
+    taken = []
+    load("fine", fine_hbm, fine, 3)
+    load("pull", pull_hbm, pull, 2)
 
     barrier = pltpu.get_barrier_semaphore()
 
@@ -196,12 +209,11 @@
 
     def roll_taps(src, b, taps, at):
         x = src[b]
-        wide = x.astype(F32)
         taps[at, 0:CH, :] = x
         for d in range(6):
             stride = STRIDES[d // 2]
-            moved = pltpu.roll(wide, stride if d % 2 == 0 else VOX - stride, 1)
-            taps[at, CH * (d + 1) : CH * (d + 2), :] = (moved * keep[d]).astype(BF16)
+            moved = pltpu.roll(x, stride if d % 2 == 0 else VOX - stride, 1)
+            taps[at, CH * (d + 1) : CH * (d + 2), :] = moved * keep[d].astype(BF16)
 
     def gather_faces(faces, land, near):
         faces[PREV0 : PREV0 + 6] = land[...]
@@ -240,17 +252,25 @@
         pltpu.make_async_copy(buf.at[pl.ds(1, count)], buf.at[pl.ds(1, count)], sem).wait()
 
     def send_rows(src, dst, back, k):
-        def body(i, carry):
+        for i in FAR_FIRST:
+            dx, dz = i // 8, i % 8
             pltpu.make_async_remote_copy(
                 src_ref=src.at[i], dst_ref=dst.at[i], send_sem=asend.at[k], recv_sem=arecv.at[k],
-                device_id=rel(n_blk - i if back else i), device_id_type=MESH,
+                device_id=apart(4 - dx, 8 - dz) if back else apart(dx, dz), device_id_type=MESH,
             ).start()
-            return carry
-
-        lax.fori_loop(1, n_blk, body, 0)
-
-    loads["fine"].wait()
-    loads["pull"].wait()
+
+    load("cot", cot_hbm, cot)
+    load("spread", spread_hbm, spread)
+    load("perm", perm_hbm, perm)
+    load("place", place_hbm, place)
+    load("up", w_up_hbm, w_up)
+    load("down", w_down_hbm, w_down)
+    load("coarse", w_coarse_hbm, w_coarse, 3)
+    load("perm_t", perm_t_hbm, perm_t)
+    load("spread_t", spread_t_hbm, spread_t)
+
+    loaded("fine")
+    loaded("pull")
     make_faces(fine, faces1, None)
     load_idx.wait()
     make_packs(faces1, pack1)
@@ -270,8 +290,9 @@
     own_row = jnp.sum(jnp.where(sub16 == lane16, own_col, 0), axis=0, keepdims=True)
     same = (own_col == own_row) & (lane16 < sub16)
     slot = jnp.sum(same.astype(jnp.int32), axis=1, keepdims=True)
-    gap = own_col[:, :1] - me_b
-    ahead = jnp.where(gap < 0, gap + n_blk, gap)
+    own_at = own_col[:, :1]
+    ahead = 8 * lax.bitwise_and(lax.shift_right_logical(own_at, 3) + 4 - me_x, 3) + (
+        lax.bitwise_and(own_at + 8 - me_z, 7))
     start = jnp.where(iota((CELLS, 1), 0) < NB, ahead * 16 + 5 * slot, -1000)
     start_col = jnp.concatenate([start + j for j in range(5)] + [start * 0 - 1000] * 3, axis=0)
     route_t = (iota((128, packet_rows), 1) == start_col).astype(BF16)
@@ -287,9 +308,9 @@
         return dot(route_pk[...], payload).astype(BF16).reshape(n_blk, 16, 128)
 
     ysum[...] = jnp.zeros((CELLS, VOX), F32)
-    loads["cot"].wait()
-    loads["spread"].wait()
-    loads["perm"].wait()
+    loaded("cot")
+    loaded("spread")
+    loaded("perm")
     d_raised = dot(octant_rows(cot).astype(BF16), perm[...]).astype(BF16)
     pk_a[...] = packets(d_raised, cell_hot)
     arr_a[0] = pk_a[0]
@@ -304,8 +325,8 @@
         pre[b] = dot(w_fwd[...], own_taps[b])
         return carry
 
-    lax.fori_loop(0, NB, own_forward, 0)
-    loads["place"].wait()
+    lax.fori_loop(0, NB, own_forward, 0, unroll=NB)
+    loaded("place")
     for copy in copies1:
         copy.wait_recv()
     gather_faces(faces1, land1, near1)
@@ -320,7 +341,7 @@
             mid[b] = (fine[b].astype(F32) + value * jax.nn.sigmoid(value)).astype(BF16)
         return carry
 
-    lax.fori_loop(0, NB // 4, fine_forward, 0)
+    lax.fori_loop(0, NB // 4, fine_forward, 0, unroll=NB // 4)
     means = dot((octant_rows(mid) * (1.0 / 64.0)).astype(BF16), perm[...]).astype(BF16)
     pk_b[...] = packets(means, jnp.zeros((CELLS, 128), F32))
     arr_b[0] = pk_b[0]
@@ -341,10 +362,10 @@
     hot_t = hot.T[:CELLS].astype(BF16)
     hot16 = hot.astype(BF16)
     raised_hi, raised_lo = two_parts(dot(hot_t, lined(arr_a)))
-    loads["up"].wait()
+    loaded("up")
     lift = dot_nt(jnp.concatenate([raised_hi, raised_lo], axis=0), w_up[...])
     dco[...] = cotc[...].astype(F32) + lift[:CELLS] + lift[CELLS:]
-    loads["down"].wait()
+    loaded("down")
 
     def rim_copies(src, dst, offsets, base):
         count = len(offsets)
@@ -413,7 +434,7 @@
     copies2 = rim_copies(rimsrc1, rim1, WIDE, 0)
     for copy in copies2:
         copy.start()
-    loads["coarse"].wait()
+    loaded("coarse")
     for copy in copies2:
         copy.wait_recv()
 
@@ -502,7 +523,7 @@
         ).astype(BF16)
         return carry
 
-    lax.fori_loop(0, 5, tap_rows, 0)
+    lax.fori_loop(0, 5, tap_rows, 0, unroll=5)
     rows_scale = 1.0 / math.sqrt(NB * total)
 
     @pl.when(me_s == n_slab - 1)
@@ -535,8 +556,8 @@
         return carry
 
     lax.fori_loop(1, n_blk // 2, send_window, 0)
-    loads["perm_t"].wait()
-    loads["spread_t"].wait()
+    loaded("perm_t")
+    loaded("spread_t")
     row_wait(rarr, arecv.at[2])
     rows = dot(route_t, rarr[...].reshape(packet_rows, 128))
     lifted = jnp.concatenate([rows[0:16], rows[16:32]], axis=1).astype(BF16)
@@ -556,7 +577,7 @@
             dpf[b] = (d_mid * (s * (1.0 + value * (1.0 - s)))).astype(BF16)
         return carry
 
-    lax.fori_loop(0, NB // 4, fine_slope, 0)
+    lax.fori_loop(0, NB // 4, fine_slope, 0, unroll=NB // 4)
     make_faces(dpf, faces2, faces_wide)
     make_packs(faces2, pack2)
     copies4 = face_copies(land2, pack2, 1)
@@ -569,7 +590,7 @@
         gacc[...] += dot_nt(own_taps[b], dpf[b])
         return carry
 
-    lax.fori_loop(0, NB, weight_grad, 0)
+    lax.fori_loop(0, NB, weight_grad, 0, unroll=NB)
     for d in range(6):
         gacc[CH * (d + 1) : CH * (d + 2), :] += dot_nt(near1[d], faces_wide[d])
     fine_bf = (gacc[...] * (1.0 / math.sqrt(NB * total * VOX))).astype(BF16)
@@ -599,7 +620,7 @@
         big[b] += dot(w_back, back_taps[buf])
         return carry
 
-    lax.fori_loop(0, NB, own_backward, 0)
+    lax.fori_loop(0, NB, own_backward, 0, unroll=NB)
     for copy in copies4:
         copy.wait_recv()
     gather_faces(faces2, land2, near2)
@@ -612,15 +633,17 @@
             grad_fine[b] = (big[b] + more[bb]).astype(BF16)
         return carry
 
-    lax.fori_loop(0, NB // 4, fine_backward, 0)
+    lax.fori_loop(0, NB // 4, fine_backward, 0, unroll=NB // 4)
     store_grad = pltpu.make_async_copy(grad_fine, grad_fine_hbm, osem.at[0])
     store_grad.start()
 
     @pl.when(me_b < 7)
     def _():
         pltpu.make_async_copy(fland, fland, vrecv.at[1]).wait()
-        unit_ref[...] = lax.fori_loop(
-            1, n_blk, lambda i, c: c + fland[i].astype(F32), fland[0].astype(F32)).astype(BF16)
+        unit_sum = fland[0].astype(F32)
+        for i in range(1, n_blk):
+            unit_sum = unit_sum + fland[i].astype(F32)
+        unit_ref[...] = unit_sum.astype(BF16)
 
     unit = me_b + 9
     low = (256 * (unit - 2) - 2304 + 502 + 503 * 8) // 503 - 8
@@ -649,12 +672,14 @@
             fine_out[b] = (mid[b].astype(F32) + spreadv[bb]).astype(BF16)
         return carry
 
-    lax.fori_loop(0, NB // 4, fine_up, 0)
+    lax.fori_loop(0, NB // 4, fine_up, 0, unroll=NB // 4)
     store_out = pltpu.make_async_copy(fine_out, fine_out_hbm, osem.at[1])
     store_out.start()
     row_wait(wland, vrecv.at[0], n_blk // 2 - 1)
-    gsum[...] = lax.fori_loop(
-        1, n_blk // 2, lambda i, c: c + wland[i].astype(F32), window_of(me_b)[...].astype(F32))
+    summed = window_of(me_b)[...].astype(F32)
+    for i in range(1, n_blk // 2):
+        summed = summed + wland[i].astype(F32)
+    gsum[...] = summed
 
     my_unit = (16 * skew + 503 * me_b) // 256
     for u in range(3):
@@ -724,7 +749,7 @@
             f32(CELLS, WID), bf(4, WID, 128), bf(5 * WID, WID), bf(n_blk // 2, 48, WID), bf(7, 16, WID),
             bf(n_blk, 16, WID), bf(16, WID), bf(3, n_slab, 16, WID), f32(48, WID),
             pltpu.VMEM((8, 128), jnp.int32), pltpu.SMEM((8, 128), jnp.int32),
-            dma((11,)), dma, dma((2,)), dma((4,)), dma((4,)), dma((3,)), dma((3,)), dma((32,)),
+            dma((16,)), dma, dma((2,)), dma((4,)), dma((4,)), dma((3,)), dma((3,)), dma((32,)),
             dma((32,)), dma((32,)), dma((4,)), dma, dma((2,)), dma((9,)), dma((3,)),
         ],
         compiler_params=pltpu.CompilerParams(
@@ -734,42 +759,44 @@
 
 
 def finish_kernel(fine_in, grad_in, coarse_in, latent_in, flat_in, fine_to, grad_to, coarse_to,
-                  latent_to, flat_to, held, in_sems, out_sems):
-    takes, gives = [], []
+                  latent_to, flat_to, held, cells, flat, in_sems, out_sems):
+    moves = [(flat_in, flat, None), (coarse_in, cells.at[0], coarse_to),
+             (latent_in, cells.at[1], latent_to)]
     for i, (src, dst) in enumerate(((fine_in, fine_to), (grad_in, grad_to))):
         for j in range(4):
             rows = pl.ds(3 * j, 3)
-            n = 4 * i + j
-            takes.append(pltpu.make_async_copy(src.at[rows], held.at[i, rows], in_sems.at[n]))
-            gives.append(pltpu.make_async_copy(held.at[i, rows], dst.at[rows], out_sems.at[n]))
+            moves.append((src.at[rows], held.at[i, rows], dst.at[rows]))
+    takes = [pltpu.make_async_copy(src, mid, in_sems.at[n])
+             for n, (src, mid, dst) in enumerate(moves)]
+    gives = [pltpu.make_async_copy(mid, dst, out_sems.at[n])
+             for n, (src, mid, dst) in enumerate(moves) if dst is not None]
     for copy in takes:
         copy.start()
-    coarse_to[...] = coarse_in[...]
-    latent_to[...] = latent_in[...]
-    for r in range(SHARD // WID):
-        flat_to[WID * r : WID * r + WID] = flat_in[r, :]
-    rest = SHARD % WID
-    flat_to[SHARD - rest : SHARD] = flat_in[SHARD // WID, :rest]
-    for take, give in zip(takes, gives):
+    for take, give in zip(takes[1:], gives):
         take.wait()
         give.start()
+    takes[0].wait()
+    for r in range(SHARD // WID):
+        flat_to[WID * r : WID * r + WID] = flat[r, :]
+    rest = SHARD % WID
+    flat_to[SHARD - rest : SHARD] = flat[SHARD // WID, :rest]
     for give in gives:
         give.wait()
 
 
 def finish(fine_out, coarse_out, grad_fine, grad_latent, flat):
     hbm = pl.BlockSpec(memory_space=pl.ANY)
-    vmem = pl.BlockSpec(memory_space=pltpu.VMEM)
     like = lambda a: jax.ShapeDtypeStruct(a.shape, a.dtype)
     fine_out, grad_fine, coarse_out, grad_latent, flat = pl.pallas_call(
         finish_kernel,
         name="finish",
         out_shape=(like(fine_out), like(grad_fine), like(coarse_out), like(grad_latent),
                    jax.ShapeDtypeStruct((SHARD,), F32)),
-        in_specs=[hbm, hbm, vmem, vmem, vmem],
-        out_specs=(hbm, hbm, vmem, vmem, vmem),
-        scratch_shapes=[pltpu.VMEM((2, NB, CH, VOX), BF16), pltpu.SemaphoreType.DMA((8,)),
-                        pltpu.SemaphoreType.DMA((8,))],
+        in_specs=[hbm] * 5,
+        out_specs=(hbm, hbm, hbm, hbm, pl.BlockSpec(memory_space=pltpu.VMEM)),
+        scratch_shapes=[pltpu.VMEM((2, NB, CH, VOX), BF16), pltpu.VMEM((2, CELLS, WID), BF16),
+                        pltpu.VMEM((32, WID), F32), pltpu.SemaphoreType.DMA((11,)),
+                        pltpu.SemaphoreType.DMA((11,))],
     )(fine_out, grad_fine, coarse_out, grad_latent, flat)
     return fine_out, coarse_out, grad_fine, grad_latent, flat
 

time: 69.5 us -> 66.1 us (0.951)
  Pallas kernels: 68.4 us -> 65.1 us
    pallas_call x1, Pallas kernels: 64.7 us -> 62.1 us  [fused(): pl.pallas_call(functools.partial(kernel, n_slab, n_blk), name='window', o...]
    pallas_call x1, Pallas kernels: 3.7 us -> 3 us  [finish(): pl.pallas_call(finish_kernel, name='finish', out_shape=(like(fine_out), l...]
where the time goes in v4:
time: 66.1 us; the launch traced here: 65.9 us
  Pallas kernels  65.1 us (98%)
  between operations  0.8 us (1%)
    pallas_call x1, Pallas kernels, fused(): pl.pallas_call(functools.partial(kernel, n_slab, n_blk), name='window', o...  62.1 us
    pallas_call x1, Pallas kernels, finish(): pl.pallas_call(finish_kernel, name='finish', out_shape=(like(fine_out), l...  3 us

profile of v4, /device:TPU:32, one launch (start us, length us, event | category | flops | bytes accessed | tf_op | source)
XLA Modules:
  0.0 65.9 jit_solution(11627382118979185242)
XLA Ops:
  0.6 62.1 %window.1 = (bf16[12,64,512]{2,1,0:T(8,128)(2,1)}, bf16[16,256]{1,0:T(8,128)(2,1)}, bf16[12,64,512]{2,1,0:T(8,128)(2,1)}, bf16[16,256]{1,0:T(8,128)(2,1)}, f32[32,256]{1,0:T(8,128)}) custom-call(bf16[12,64,512]{2,1,0:T(8,128)(2,1)} %fine_hbm.1, bf16[12,64,512]{2,1,0:T(8,128)(2,1)} %cot_hbm.1, bf16[16,256]{1,0:T(8,128)(2,1)} %bitcast.8, ...), custom_call_target="tpu_custom_call" | custom-call | tf_op jit(solution)/shard_map/window/pallas_call | solution.py:727
  62.7 3.0 %finish.1 = (bf16[12,64,512]{2,1,0:T(8,128)(2,1)}, bf16[12,64,512]{2,1,0:T(8,128)(2,1)}, bf16[16,256]{1,0:T(8,128)(2,1)}, bf16[16,256]{1,0:T(8,128)(2,1)}, f32[8048]{0:T(1024)}) custom-call(bf16[12,64,512]{2,1,0:T(8,128)(2,1)} %get-tuple-element.15.fine_in, bf16[12,64,512]{2,1,0:T(8,128)(2,1)} %get-tuple-element.16.grad_in, ...), custom_call_target="tpu_custom_call" | custom-call | tf_op jit(solution)/shard_map/finish/pallas_call | solution.py:790

commit v5 on v4

--- a/solution.py
+++ b/solution.py
@@ -81,7 +81,7 @@
     fine_out_hbm, coarse_out, grad_fine_hbm, grad_latent, grads_out,
     fine, cot, w_down, w_up, w_coarse, pull, place, spread, spread_t, perm, perm_t,
     fine_out, grad_fine, faces1, faces2, faces_wide, pack1, pack2, land1, land2, half, near1, near2, zall,
-    own_taps, back_taps, pre, mid, dpf, big, ysum, yrow, w_bwd, route_pk, arr_a, arr_b, pk_a, pk_b, rpk, rarr,
+    own_taps, back_taps, pre, mid, dpf, big, ysum, yrow, w_bwd, route_pk, cells_of, arr_a, arr_b, pk_a, pk_b, rpk, rarr,
     rim1, rim2, rimsrc1, rimsrc2, triple, boxes, d_box, d_all, gacc, xsrc, dsrc, upsrc, downsrc, xgat, dgat, upgat, downgat,
     dco, xq, gbuf, wland, fsrc, fland, unit_ref, uland, gsum, idx_v, idx_s,
     wsem, isem, osem, fsend, frecv, asend, arecv, rsend, rrecv, csend, crecv, vsend, vrecv,
@@ -347,9 +347,9 @@
     arr_b[0] = pk_b[0]
     send_rows(pk_b, arr_b, False, 1)
 
-    def lined(arr):
-        wide = arr[...].reshape(packet_rows, 128).astype(F32)
-        return jnp.concatenate([pltpu.roll(wide, 4 - j, 0) for j in range(4)], axis=1).astype(BF16)
+    def by_cell(arr):
+        parts = dot(cell_pick, arr[...].reshape(packet_rows, 128))
+        return jnp.concatenate([parts[16 * j : 16 * j + 16] for j in range(4)], axis=1)
 
     def two_parts(x):
         high = x.astype(BF16)
@@ -359,9 +359,12 @@
     row_of = iota((packet_rows, 128), 0) % 16
     hot = jnp.where(
         (row_of == 4) | (row_of == 9), arr_a[...].reshape(packet_rows, 128).astype(F32), 0.0)
-    hot_t = hot.T[:CELLS].astype(BF16)
-    hot16 = hot.astype(BF16)
-    raised_hi, raised_lo = two_parts(dot(hot_t, lined(arr_a)))
+    cell_rows = jnp.zeros((packet_rows, 128), F32)
+    for j in range(4):
+        cell_rows = cell_rows + pltpu.roll(pltpu.roll(hot, packet_rows - 4 + j, 0), 16 * j, 1)
+    cell_pick = cell_rows.T[:64].astype(BF16)
+    cells_of[...] = cell_rows.astype(BF16)
+    raised_hi, raised_lo = two_parts(by_cell(arr_a))
     loaded("up")
     lift = dot_nt(jnp.concatenate([raised_hi, raised_lo], axis=0), w_up[...])
     dco[...] = cotc[...].astype(F32) + lift[:CELLS] + lift[CELLS:]
@@ -388,7 +391,7 @@
     for copy in copies3:
         copy.start()
     row_wait(arr_b, arecv.at[1])
-    means_hi, means_lo = two_parts(dot(hot_t, lined(arr_b)))
+    means_hi, means_lo = two_parts(by_cell(arr_b))
     pooled = dot(jnp.concatenate([means_hi, means_lo], axis=0), w_down[...])
     c_in = (latent[...].astype(F32) + pooled[:CELLS] + pooled[CELLS:]).astype(BF16)
 
@@ -488,13 +491,9 @@
     g_lat = (dco[...] + acc).astype(BF16)
     grad_latent[...] = g_lat
 
-    grid = jnp.concatenate([c_out.astype(F32), g_lat.astype(F32)], axis=1)
-    grid = jnp.concatenate([grid, jnp.zeros((128 - CELLS, 2 * WID), F32)], axis=0).astype(BF16)
-    picked = dot(hot16, grid)
-    back = jnp.zeros((packet_rows, 128), F32)
-    for j in range(4):
-        back = back + pltpu.roll(picked[:, 128 * j : 128 * j + 128], packet_rows - 4 + j, 0)
-    rpk[...] = back.astype(BF16).reshape(n_blk, 16, 128)
+    halves = [x[:, at : at + 128].astype(F32) for x in (c_out, g_lat) for at in (0, 128)]
+    grid = jnp.concatenate(halves + [jnp.zeros((64, 128), F32)], axis=0).astype(BF16)
+    rpk[...] = dot(cells_of[...], grid).astype(BF16).reshape(n_blk, 16, 128)
     rarr[0] = rpk[0]
     send_rows(rpk, rarr, True, 2)
     downsrc[...] = jnp.concatenate([g_lat.astype(F32), means_hi.astype(F32)], axis=1).astype(BF16)
@@ -739,7 +738,7 @@
             bf(6, CH, 128), bf(2, CH, 128), bf(6, CH, NB * 128), bf(6, CH, NB * 128),
             bf(NB, CH, 6 * 128), bf(NB, 7 * CH, VOX), bf(2, 7 * CH, VOX), f32(NB, CH, VOX), bf(NB, CH, VOX), bf(NB, CH, VOX),
             f32(NB, CH, VOX), f32(CELLS, VOX), f32(CELLS, VOX), f32(CH, 7 * CH),
-            bf(n_blk * 16, 128), bf(*rows), bf(*rows), bf(*rows), bf(*rows), bf(*rows), bf(*rows),
+            bf(n_blk * 16, 128), bf(n_blk * 16, 128), bf(*rows), bf(*rows), bf(*rows), bf(*rows), bf(*rows), bf(*rows),
             bf(24, CELLS, WID), f32(8, CELLS, WID), bf(CELLS, WID), f32(CELLS, WID),
             bf(25, CELLS, 3 * WID), f32(9 * CELLS, WID), f32(9, CELLS, WID), bf(WID, WID),
             f32(7 * CH, CH),
@@ -772,14 +771,14 @@
              for n, (src, mid, dst) in enumerate(moves) if dst is not None]
     for copy in takes:
         copy.start()
-    for take, give in zip(takes[1:], gives):
-        take.wait()
-        give.start()
     takes[0].wait()
     for r in range(SHARD // WID):
         flat_to[WID * r : WID * r + WID] = flat[r, :]
     rest = SHARD % WID
     flat_to[SHARD - rest : SHARD] = flat[SHARD // WID, :rest]
+    for take, give in zip(takes[1:], gives):
+        take.wait()
+        give.start()
     for give in gives:
         give.wait()
 

time: 66.1 us -> 66.1 us (level)
  no operation moved by 1% of the time
where the time goes in v5:
time: 66.1 us; the launch traced here: 65.9 us
  Pallas kernels  65.1 us (98%)
  between operations  0.8 us (1%)
    pallas_call x1, Pallas kernels, fused(): pl.pallas_call(functools.partial(kernel, n_slab, n_blk), name='window', o...  62.1 us
    pallas_call x1, Pallas kernels, finish(): pl.pallas_call(finish_kernel, name='finish', out_shape=(like(fine_out), l...  3 us

profile of v5, /device:TPU:32, one launch (start us, length us, event | category | flops | bytes accessed | tf_op | source)
XLA Modules:
  0.0 65.9 jit_solution(4924106504193235210)
XLA Ops:
  0.6 62.1 %window.1 = (bf16[12,64,512]{2,1,0:T(8,128)(2,1)}, bf16[16,256]{1,0:T(8,128)(2,1)}, bf16[12,64,512]{2,1,0:T(8,128)(2,1)}, bf16[16,256]{1,0:T(8,128)(2,1)}, f32[32,256]{1,0:T(8,128)}) custom-call(bf16[12,64,512]{2,1,0:T(8,128)(2,1)} %fine_hbm.1, bf16[12,64,512]{2,1,0:T(8,128)(2,1)} %cot_hbm.1, bf16[16,256]{1,0:T(8,128)(2,1)} %bitcast.8, ...), custom_call_target="tpu_custom_call" | custom-call | tf_op jit(solution)/shard_map/window/pallas_call | solution.py:726
  62.7 3.0 %finish.1 = (bf16[12,64,512]{2,1,0:T(8,128)(2,1)}, bf16[12,64,512]{2,1,0:T(8,128)(2,1)}, bf16[16,256]{1,0:T(8,128)(2,1)}, bf16[16,256]{1,0:T(8,128)(2,1)}, f32[8048]{0:T(1024)}) custom-call(bf16[12,64,512]{2,1,0:T(8,128)(2,1)} %get-tuple-element.15.fine_in, bf16[12,64,512]{2,1,0:T(8,128)(2,1)} %get-tuple-element.16.grad_in, ...), custom_call_target="tpu_custom_call" | custom-call | tf_op jit(solution)/shard_map/finish/pallas_call | solution.py:789
